TPU v7x, 256 devices: a whole 4x4x8 slice. The times are simulated.
256 devices in a mesh: dp: 4 (over y), expert: 64 (over z, x, core).
Axes of the slice: x: 4, y: 4, z: 8, core: 2. Of those that a mesh axis runs over, the one named last changes fastest.
Arguments:
- out_grad: bfloat16 [40960, 3584], P('expert', 'dp'), may hold values from -0.3125 to 0.3125
- routes: int32 [40960, 4], P('expert'), may hold values from 0 to 127, all different within a row; in each aligned block of 640 rows (0 to 639, 640 to 1279, ...) at most 30 rows name the same one
- gates: float32 [40960, 4], P('expert'), may hold values from 0.05 to 1
- dup_owner: int32 [64], replicated, may hold values from 0 to 63
- hidden: bfloat16 [64, 64, 2, 30, 1024], P('expert', None, None, None, 'dp'), may hold values from -6 to 6
- moment1: bfloat16 [64, 1024, 3584], P(None, 'expert', 'dp'), may hold values from -0.625 to 0.625
- moment2: bfloat16 [64, 1024, 3584], P(None, 'expert', 'dp'), may hold values from 0.0099487305 to 0.29882812
- value_grad: bfloat16 [40960, 4096], P('expert', 'dp'), may hold values from -2 to 2
- value_proj: bfloat16 [512, 4096], P(None, 'dp'), may hold values from -0.25 to 0.25
Outputs:
- slot_steps: bfloat16 [64, 2, 1024, 3584], P('expert', None, None, 'dp')
- latent_grad: bfloat16 [512, 40960], P('dp', 'expert')
Inputs may be any that keep to these rules, and one draw needn't show every extreme that they name: Among the routes of one token group's rows, a token names distinct slots, a slot is named at most 30 times, a bound that some block reaches.
All inputs are finite; a program needn't handle non-finite values.
Results may differ from a plain program's by a relative error of at most 0.0065.
Values may be sent and summed in bfloat16 or wider, within the bound.
A program may use at most 128 MiB of HBM per device.

v0:
```python
import jax
import jax.numpy as jnp
from jax import lax
from jax.sharding import PartitionSpec as P

beta_first = 0.9
beta_second = 0.95
adam_eps = 1e-08
bias_first = 1.0 - 0.9**50 * 0.9**50
bias_second = 1.0 - 0.95**50 * 0.95**50


def shards(out_grad, routes, gates, dup_owner, hidden, moment1, moment2, value_grad, value_proj):
    groups = lax.axis_size("expert")
    per_token = routes.shape[1]
    slot_total = 2 * groups
    capacity = hidden.shape[3]
    width_part = out_grad.shape[1]
    flat_routes = routes.reshape(-1)
    onehot = (flat_routes[:, None] == jnp.arange(slot_total, dtype=jnp.int32)[None, :]).astype(
        jnp.int32
    )
    route_rank = jnp.sum((jnp.cumsum(onehot, axis=0) - onehot) * onehot, axis=1)
    target = flat_routes * capacity + route_rank
    scaled = (gates.reshape(-1, 1) * jnp.repeat(out_grad, per_token, axis=0)).astype(jnp.bfloat16)
    outgoing = jnp.zeros((slot_total * capacity, width_part), jnp.bfloat16).at[target].set(scaled)
    outgoing = outgoing.reshape(groups, 2, capacity, width_part)
    local_hidden = hidden[0]
    arrived = lax.all_to_all(outgoing, "expert", split_axis=0, concat_axis=0, tiled=True)

    def one_slot(piece_slot, slot_index):
        return jnp.einsum(
            "scf,scd->fd", piece_slot, arrived[:, slot_index], preferred_element_type=jnp.float32
        )

    piece = lax.all_gather(local_hidden, "dp", axis=3, tiled=True)
    partial_value = jnp.stack([one_slot(piece[:, 0], 0), one_slot(piece[:, 1], 1)], axis=0)
    arrived_parts = lax.all_to_all(partial_value, "expert", split_axis=1, concat_axis=1, tiled=True)
    rows_each = arrived_parts.shape[1] // groups
    pieces = arrived_parts.reshape(2, groups, rows_each, width_part)
    owner_table = (dup_owner[:, None] == jnp.arange(groups, dtype=jnp.int32)[None, :]).astype(
        jnp.float32
    )
    gradient = pieces[0] + jnp.einsum(
        "se,sfd->efd", owner_table, pieces[1], precision=lax.Precision.HIGHEST
    )
    first_moment = beta_first * moment1.astype(jnp.float32) + (1.0 - beta_first) * gradient
    second_moment = (
        beta_second * moment2.astype(jnp.float32) + (1.0 - beta_second) * gradient * gradient
    )
    expert_step = (
        first_moment / bias_first / (jnp.sqrt(second_moment / bias_second) + adam_eps)
    ).astype(jnp.bfloat16)
    outgoing_steps = jnp.stack([expert_step, expert_step[dup_owner]], axis=0)
    returned = lax.all_to_all(outgoing_steps, "expert", split_axis=1, concat_axis=1, tiled=True)
    slot_steps = returned.reshape(1, 2, groups * rows_each, width_part)
    latent_grad = lax.psum_scatter(
        lax.dot_general(
            value_proj, value_grad, (((1,), (1,)), ((), ())), preferred_element_type=jnp.float32
        ),
        "dp",
        scatter_dimension=0,
        tiled=True,
    ).astype(jnp.bfloat16)
    return (slot_steps, latent_grad)


def solution(mesh):
    in_specs = (
        P("expert", "dp"),
        P("expert", None),
        P("expert", None),
        P(),
        P("expert", None, None, None, "dp"),
        P(None, "expert", "dp"),
        P(None, "expert", "dp"),
        P("expert", "dp"),
        P(None, "dp"),
    )
    out_specs = (P("expert", None, None, "dp"), P("dp", "expert"))
    return jax.shard_map(shards, mesh=mesh, in_specs=in_specs, out_specs=out_specs, check_vma=False)
```

profile of v0, /device:TPU:1, one launch (start us, length us, event | category | flops | bytes accessed | tf_op | source)
XLA Modules:
  0.0 579.7 jit_solution(6225343921767255426)
XLA Ops:
  7.2 1.0 copy.55
  8.6 0.7 broadcast_multiply_fusion
  10.7 6.0 %broadcast_in_dim.14 = f32[640,4,896]{2,1,0:T(4,128)} broadcast(bf16[640,896]{1,0:T(8,128)(2,1)} %param.9), dimensions={0,2} | broadcast | bytes 10321920 | tf_op jit(solution)/shard_map/broadcast_in_dim | solution.py:25
  16.7 11.6 %convert_element_type.34 = f32[2560,896]{1,0:T(8,128)} reshape(f32[640,4,896]{2,1,0:T(4,128)} %broadcast_in_dim.14) | data formatting | bytes 18350080 | tf_op jit(solution)/shard_map/convert_element_type | solution.py:25
  28.6 1.6 fusion.20
  30.3 17.7 %scatter_custom_fusion = bf16[3840,896]{1,0:T(8,128)(2,1)} fusion(s32[2560]{0:T(1024)S(1)} %fusion.25, f32[2560,896]{1,0:T(8,128)} %convert_element_type.34, f32[2560]{0:T(1024)S(1)} %mul.62, bf16[]{:T(256)} %constant.13.clone.1), kind=kCustom, calls=%fused_computation.5 | custom fusion | flops 4587520 | bytes 16068610 | tf_op jit(solution)/shard_map/scatter | solution.py:26
  48.0 10.0 %reshape.67 = bf16[64,2,30,896]{3,2,1,0:T(8,128)(2,1)} reshape(bf16[3840,896]{1,0:T(8,128)(2,1)} %scatter_custom_fusion) | data formatting | bytes 13762560 | tf_op jit(solution)/shard_map/reshape | solution.py:27
  58.0 11.3 %copy.60 = bf16[64,2,30,896]{3,1,2,0:T(2,128)(2,1)} copy(bf16[64,2,30,896]{3,2,1,0:T(8,128)(2,1)} %reshape.67) | data formatting | bytes 13762560 | tf_op jit(solution)/shard_map/reshape | solution.py:27
  69.3 13.3 %all-to-all-start = ((bf16[64,2,30,896]{3,1,2,0:T(2,128)(2,1)}), bf16[64,2,30,896]{3,1,2,0:T(2,128)(2,1)}, u32[]{:S(2)}, u32[]{:S(2)}) async-start(bf16[64,2,30,896]{3,1,2,0:T(2,128)(2,1)} %copy.60), calls=%async_computation | async-start | bytes 13762560 | tf_op jit(solution)/shard_map/all_to_all | solution.py:29
  82.6 1.6 copy.62
  84.3 149.0 %all-to-all-done = bf16[64,2,30,896]{3,1,2,0:T(2,128)(2,1)} async-done(((bf16[64,2,30,896]{3,1,2,0:T(2,128)(2,1)}), bf16[64,2,30,896]{3,1,2,0:T(2,128)(2,1)}, u32[]{:S(2)}, u32[]{:S(2)}) %all-to-all-start) | async-done | bytes 6881312 | tf_op jit(solution)/shard_map/all_to_all | solution.py:29
  233.3 14.8 %fusion.27 = (bf16[64,1,30,896]{3,1,2,0:T(2,128)(2,1)}, bf16[64,1,30,896]{3,1,2,0:T(2,128)(2,1)}) fusion(bf16[64,2,30,896]{3,1,2,0:T(2,128)(2,1)} %all-to-all-done), kind=kLoop, calls=%fused_computation.46 | loop fusion | bytes 13762560 | tf_op jit(solution)/shard_map/slice | solution.py:33
  248.2 8.2 %fusion.15 = f32[1,1024,896]{1,2,0:T(8,128)S(1)} fusion(bf16[64,2,30,1024]{3,0,2,1:T(8,128)(2,1)} %bitcast.62, bf16[64,1,30,896]{3,1,2,0:T(2,128)(2,1)} %get-tuple-element.4), kind=kOutput, calls=%fused_computation.24 | convolution fusion | flops 3523215360 | bytes 14483456 | tf_op jit(solution)/shard_map/scf,scd->fd/dot_general | solution.py:32
  256.4 4.0 fusion.16
  260.4 4.4 pad_maximum_fusion
  264.9 11.9 %copy.64 = f32[2,1024,896]{2,0,1:T(2,128)} copy(f32[2,1024,896]{1,2,0:T(8,128)} %pad_maximum_fusion) | data formatting | bytes 14680064 | tf_op jit(solution)/shard_map/stack | solution.py:37
  276.7 9.2 %all-to-all-start.1 = ((f32[2,1024,896]{2,0,1:T(2,128)}), f32[2,1024,896]{2,0,1:T(2,128)}, u32[]{:S(2)}, u32[]{:S(2)}) async-start(f32[2,1024,896]{2,0,1:T(2,128)} %copy.64), calls=%async_computation.1 | async-start | bytes 14680064 | tf_op jit(solution)/shard_map/all_to_all | solution.py:38
  285.9 160.3 %all-to-all-done.1 = f32[2,1024,896]{2,0,1:T(2,128)} async-done(((f32[2,1024,896]{2,0,1:T(2,128)}), f32[2,1024,896]{2,0,1:T(2,128)}, u32[]{:S(2)}, u32[]{:S(2)}) %all-to-all-start.1) | async-done | bytes 7340064 | tf_op jit(solution)/shard_map/all_to_all | solution.py:38
  446.2 8.2 %fusion.26 = (f32[1,1024,896]{2,0,1:T(1,128)S(1)}, f32[1,1024,896]{2,0,1:T(1,128)S(1)}) fusion(f32[2,1024,896]{2,0,1:T(2,128)} %all-to-all-done.1), kind=kLoop, calls=%fused_computation.45 | loop fusion | bytes 14680064 | tf_op jit(solution)/shard_map/slice | solution.py:45
  455.0 1.2 copy-done.5
  456.2 0.6 copy-done.6
  456.8 6.6 %fusion.11 = bf16[64,16,896]{2,0,1:T(8,128)(2,1)S(1)} fusion(f32[64,16,896]{2,1,0:T(8,128)S(1)} %bitcast.59, f32[64,16,896]{2,1,0:T(8,128)S(1)} %bitcast.60, bf16[64,16,896]{2,1,0:T(8,128)(2,1)S(1)} %copy-done.5, bf16[64,16,896]{2,1,0:T(8,128)(2,1)S(1)} %copy-done.6, s32[64]{0:T(128)S(1)} %copy-done.8), kind=kOutput, calls=%fused_computation.20 | convolution fusion | flops 718409728 | bytes 12845312 | tf_op jit(solution)/shard_map/se,sfd->efd/dot_general | solution.py:44
  463.3 2.3 copy.70
  465.6 3.5 gather_fusion
  469.1 1.9 copy.98
  471.4 3.9 copy.72
  475.3 9.6 %all-to-all-start.2 = ((bf16[2,64,16,896]{3,2,0,1:T(8,128)(2,1)}), bf16[2,64,16,896]{3,2,0,1:T(8,128)(2,1)}, u32[]{:S(2)}, u32[]{:S(2)}) async-start(bf16[2,64,16,896]{3,2,0,1:T(8,128)(2,1)} %copy.72), calls=%async_computation.2 | async-start | bytes 7340032 | tf_op jit(solution)/shard_map/all_to_all | solution.py:55
  485.0 2.1 fusion.28
  487.1 28.3 %reduce-scatter.2.cloned.1.call-done = f32[128,640]{1,0:T(8,128)} async-done(((f32[512,640]{1,0:T(8,128)}), f32[128,640]{1,0:T(8,128)}) %reduce-scatter.2.cloned.1.call-update) | async-done | bytes 327696 | tf_op jit(solution)/shard_map/reduce_scatter | solution.py:57
  515.4 1.7 convert_element_type.38
  517.1 51.6 %all-to-all-done.2 = bf16[2,64,16,896]{3,2,0,1:T(8,128)(2,1)} async-done(((bf16[2,64,16,896]{3,2,0,1:T(8,128)(2,1)}), bf16[2,64,16,896]{3,2,0,1:T(8,128)(2,1)}, u32[]{:S(2)}, u32[]{:S(2)}) %all-to-all-start.2) | async-done | bytes 3670048 | tf_op jit(solution)/shard_map/all_to_all | solution.py:55
  568.7 4.2 copy.73
  (39 shorter events, 3.2 us)
Async XLA Ops:
  7.2 477.8 %copy-start = (bf16[640,1024]{1,0:T(8,128)(2,1)S(1)}, bf16[640,1024]{1,0:T(8,128)(2,1)}, u32[]{:S(2)}) copy-start(bf16[640,1024]{1,0:T(8,128)(2,1)} %param.16) | copy-start | bytes 3932164
  16.7 11.6 %copy-start.3 = (f32[640,4]{0,1:T(4,128)S(1)}, f32[640,4]{0,1:T(4,128)}, u32[]{:S(2)}) copy-start(f32[640,4]{0,1:T(4,128)} %param.11) | copy-start | bytes 30724
  69.3 13.4 %copy-start.2 = (bf16[1,64,2,30,256]{4,2,3,1,0:T(2,128)(2,1)S(1)}, bf16[1,64,2,30,256]{4,2,3,1,0:T(2,128)(2,1)}, u32[]{:S(2)}) copy-start(bf16[1,64,2,30,256]{4,2,3,1,0:T(2,128)(2,1)} %param.13) | copy-start | bytes 5898244
  69.3 164.0 %all-to-all-start = ((bf16[64,2,30,896]{3,1,2,0:T(2,128)(2,1)}), bf16[64,2,30,896]{3,1,2,0:T(2,128)(2,1)}, u32[]{:S(2)}, u32[]{:S(2)}) async-start(bf16[64,2,30,896]{3,1,2,0:T(2,128)(2,1)} %copy.60), calls=%async_computation | async-start | bytes 13762560 | tf_op jit(solution)/shard_map/all_to_all | solution.py:29
  82.6 165.6 %all-gather.3.cloned.1.call-start = ((), (), s32[]{:S(2)}) async-start(), calls=%async_computation.5 | async-start | bytes 9830400 | tf_op jit(solution)/shard_map/all_gather | solution.py:36
  248.1 8.3 %copy-start.1 = (bf16[64,1,30,896]{3,1,2,0:T(2,128)(2,1)S(1)}, bf16[64,1,30,896]{3,1,2,0:T(2,128)(2,1)}, u32[]{:S(2)}) copy-start(bf16[64,1,30,896]{3,1,2,0:T(2,128)(2,1)} %get-tuple-element.5) | copy-start | bytes 10321924
  248.2 8.3 %copy-start.4 = (bf16[1,64,2,30,1024]{4,1,3,2,0:T(8,128)(2,1)S(1)}, bf16[1,64,2,30,1024]{4,1,3,2,0:T(8,128)(2,1)}, u32[]{:S(2)}) copy-start(bf16[1,64,2,30,1024]{4,1,3,2,0:T(8,128)(2,1)} %all-gather.3.cloned.1.call-done) | copy-start | bytes 23592964
  276.7 9.2 %copy-start.8 = (s32[64]{0:T(128)S(1)}, s32[64]{0:T(128)}, u32[]{:S(2)}) copy-start(s32[64]{0:T(128)} %param.12) | copy-start | bytes 772
  276.7 169.5 %all-to-all-start.1 = ((f32[2,1024,896]{2,0,1:T(2,128)}), f32[2,1024,896]{2,0,1:T(2,128)}, u32[]{:S(2)}, u32[]{:S(2)}) async-start(f32[2,1024,896]{2,0,1:T(2,128)} %copy.64), calls=%async_computation.1 | async-start | bytes 14680064 | tf_op jit(solution)/shard_map/all_to_all | solution.py:38
  454.7 1.5 copy-start.5
  454.7 2.0 copy-start.6
  475.3 9.7 %copy-start.7 = (bf16[512,1024]{1,0:T(8,128)(2,1)S(1)}, bf16[512,1024]{1,0:T(8,128)(2,1)}, u32[]{:S(2)}) copy-start(bf16[512,1024]{1,0:T(8,128)(2,1)} %param.17) | copy-start | bytes 3145732
  475.3 93.4 %all-to-all-start.2 = ((bf16[2,64,16,896]{3,2,0,1:T(8,128)(2,1)}), bf16[2,64,16,896]{3,2,0,1:T(8,128)(2,1)}, u32[]{:S(2)}, u32[]{:S(2)}) async-start(bf16[2,64,16,896]{3,2,0,1:T(8,128)(2,1)} %copy.72), calls=%async_computation.2 | async-start | bytes 7340032 | tf_op jit(solution)/shard_map/all_to_all | solution.py:55
  484.9 30.5 %reduce-scatter.2.cloned.1.call-start = ((), (), s32[]{:S(2)}) async-start(), calls=%async_computation.4 | async-start | bytes 1638400 | tf_op jit(solution)/shard_map/reduce_scatter | solution.py:57
Sparse Core Ops, SparseCore 0:
  85.8 85.4 all-gather.2
  488.3 27.0 reduce-scatter.1
where the time goes:
time: 581 us; the launch traced here: 580 us
  waiting for transfers between devices  389 us (67%)
  local copies, waits for them, and re-layouts  95.9 us (17%)
  starting transfers between devices  32.2 us (6%)
  other arithmetic  27.1 us (5%)
  matrix products  20.9 us (4%)
  between operations  14.3 us (2%)
    all_to_all x1, waiting for transfers between devices, shards(): lax.all_to_all(partial_value, 'expert', split_axis=1, concat_axis=1, tile...  160 us
    all_to_all x1, waiting for transfers between devices, shards(): lax.all_to_all(outgoing, 'expert', split_axis=0, concat_axis=0, tiled=True)  149 us
    all_to_all x1, waiting for transfers between devices, shards(): lax.all_to_all(outgoing_steps, 'expert', split_axis=1, concat_axis=1, til...  51.6 us
    reduce_scatter x1, waiting for transfers between devices, shards(): lax.psum_scatter(lax.dot_general(value_proj, value_grad, (((1,), (1,)), (...  28.3 us
    reshape x2, local copies, waits for them, and re-layouts, shards(): outgoing = outgoing.reshape(groups, 2, capacity, width_part)  21.3 us
    scatter x1, other arithmetic, shards(): jnp.zeros((slot_total * capacity, width_part), jnp.bfloat16).at[target]  17.7 us
    slice x1, local copies, waits for them, and re-layouts, one_slot(): arrived[:, slot_index]  14.8 us
    all_to_all x1, starting transfers between devices, shards(): lax.all_to_all(outgoing, 'expert', split_axis=0, concat_axis=0, tiled=True)  13.3 us
  transfers between devices with their start and end apart: 5, of which 4 were waited for; matrix products, arithmetic and copies ran while one was open for 3% of the time, Pallas kernels for 0%

commit v1 on v0

v1 whole, which is shorter than its diff:
```python
import functools

import jax
import jax.numpy as jnp
from jax import lax
from jax.experimental import pallas as pl
from jax.experimental.pallas import tpu as pltpu
from jax.sharding import PartitionSpec as P

beta_first = 0.9
beta_second = 0.95
adam_eps = 1e-08
bias_first = 1.0 - 0.9**50 * 0.9**50
bias_second = 1.0 - 0.95**50 * 0.95**50

PLANES = 8
PEERS = 8
ROWS = 16
POS = 32
TOKENS = 640
FPART = 256
WIDTH = 896
CHUNKS = ((0, 256), (256, 256), (512, 256), (768, 128))
N = len(CHUNKS)
HALF = TOKENS // 2
MESH = pl.DeviceIdType.MESH
F32 = jnp.float32
BF16 = jnp.bfloat16


def kernel(
    og,
    meta,
    hid,
    trow,
    m1,
    m2,
    out,
    *refs,
):
    relay_x, relay_s, refs = refs[:N], refs[N : 2 * N], refs[2 * N :]
    tok, refs = refs[:N], refs[N:]
    rows_in, refs = refs[:N], refs[N:]
    grad_in, refs = refs[:N], refs[N:]
    (
        metas,
        onehot,
        gate_col,
        rows_out,
        hid_t,
        part_out,
        step_out,
        mom,
        kron,
        kron_t,
        sem_meta,
        sem_ring,
        sem_hid,
        sem_rows,
        sem_px,
        sem_pz,
        sem_sz,
        sem_sx,
        sem_local,
        sem_own,
    ) = refs
    me = lax.axis_index("expert")
    y = lax.axis_index("dp")
    z = me // PEERS
    p = me % PEERS

    def plane(d):
        return lax.rem(z + d + PLANES, PLANES)

    def peer(d):
        return lax.rem(p + d + PEERS, PEERS)

    def dev_z(to):
        return {"expert": to * PEERS + p}

    def dev_p(to):
        return {"expert": z * PEERS + to}

    def dev_y(d):
        return {"dp": lax.rem(y + d + 4, 4)}

    def remote(src, dst, sems, index_out, index_in, device):
        return pltpu.make_async_remote_copy(
            src_ref=src,
            dst_ref=dst,
            send_sem=sems.at[(0,) + index_out],
            recv_sem=sems.at[(1,) + index_in],
            device_id=device,
            device_id_type=MESH,
        )

    def others(body):
        def step(i, carry):
            body(i)
            return carry

        lax.fori_loop(1, 8, step, 0)

    barrier = pltpu.get_barrier_semaphore()

    def greet(i):
        pl.semaphore_signal(barrier, inc=1, device_id=dev_z(plane(i)), device_id_type=MESH)
        pl.semaphore_signal(barrier, inc=1, device_id=dev_p(peer(i)), device_id_type=MESH)

    others(greet)
    for d in (1, -1):
        pl.semaphore_signal(barrier, inc=1, device_id=dev_y(d), device_id_type=MESH)

    def local(src, dst, index):
        return pltpu.make_async_copy(src, dst, sem_local.at[index])

    own_tok = [
        local(og.at[:, pl.ds(CHUNKS[k][0], CHUNKS[k][1])], tok[k].at[z], k) for k in range(N)
    ]
    load_hid = local(hid, rows_out.at[1], N)
    load_meta = local(meta, metas.at[z], N + 1)

    def load_moments(k):
        c0, dc = CHUNKS[k]
        return [
            local(
                m.at[:, pl.ds(c0, dc)],
                mom.at[k % 2, i, :, pl.ds(0, dc)],
                N + 2 + 2 * (k % 2) + i,
            )
            for i, m in enumerate((m1, m2))
        ]

    load_hid.start()
    load_meta.start()
    for copy in own_tok:
        copy.start()
    for k in (0, 1):
        for copy in load_moments(k):
            copy.start()

    pl.semaphore_wait(barrier, 16)

    def meta_copy(i):
        return remote(meta, metas.at[z], sem_meta, (i,), (i,), dev_z(plane(i)))

    others(lambda i: meta_copy(i).start())

    def ring_send(k, way, step, half):
        c0, dc = CHUNKS[k]
        sign = 1 - 2 * way
        block = plane(-sign * (step - 1))
        rows = pl.ds(half * HALF, HALF)
        source = og.at[rows, pl.ds(c0, dc)] if step == 1 else tok[k].at[block, rows]
        index = (k, way, step - 1, half)
        return remote(
            source, tok[k].at[block, rows], sem_ring, index, index, dev_z(plane(sign))
        )

    def ring_arrival(k, way, step, half):
        sign = 1 - 2 * way
        block = plane(-sign * step)
        rows = pl.ds(half * HALF, HALF)
        index = (k, way, step - 1, half)
        view = tok[k].at[block, rows]
        return remote(view, view, sem_ring, index, index, dev_z(plane(sign)))

    def ring_parts(step):
        return [(way, half) for half in (0, 1) for way in (0, 1) if step < 4 or half == way]

    def ring_begin(k):
        for way, half in ring_parts(1):
            ring_send(k, way, 1, half).start()

    ring_begin(0)

    load_hid.wait()

    def transpose_piece(i, carry):
        w = i // PEERS
        q = lax.rem(i, PEERS)
        piece = rows_out[1, q, w].reshape(PLANES * POS, FPART)
        hid_t[w, y, q] = piece.T
        return carry

    lax.fori_loop(0, 2 * PEERS, transpose_piece, 0)

    def hid_copy(index, w, part, d):
        view = hid_t.at[w, part]
        return remote(view, view, sem_hid, (index,), (index,), dev_y(d))

    def y_part(d):
        return lax.rem(y + d + 4, 4)

    hid_first = [(0, 0, 1), (1, 1, 1), (2, 0, -1), (3, 1, -1)]
    for index, w, d in hid_first:
        hid_copy(index, w, y, d).start()

    load_meta.wait()
    others(lambda i: remote(meta, metas.at[plane(-i)], sem_meta, (i,), (i,), dev_z(z)).wait_recv())
    earlier = (
        lax.broadcasted_iota(jnp.int32, (TOKENS, TOKENS), 0)
        < lax.broadcasted_iota(jnp.int32, (TOKENS, TOKENS), 1)
    ).astype(F32).astype(BF16)

    def build_plane(i, carry):
        slot_of = (lax.broadcasted_iota(jnp.int32, (16, TOKENS), 0) + z * 16).astype(F32)
        named = jnp.zeros((16, TOKENS), F32)
        gate = jnp.zeros((16, TOKENS), F32)
        table = metas[i]
        for k in range(4):
            match = slot_of == table[k : k + 1, :]
            named = jnp.where(match, 1.0, named)
            gate = jnp.where(match, table[4 + k : 5 + k, :], gate)
        rank = jnp.dot(named.astype(BF16), earlier, preferred_element_type=F32)
        rank = jnp.where(named > 0.5, rank, -1.0)
        position = lax.broadcasted_iota(jnp.int32, (POS, TOKENS), 0).astype(F32)
        for s in range(16):
            chosen = position == rank[s : s + 1, :]
            onehot[i, s * POS : (s + 1) * POS, :] = jnp.where(chosen, 1.0, 0.0).astype(BF16)
            weight = jnp.sum(
                jnp.where(chosen, gate[s : s + 1, :], 0.0), axis=1, keepdims=True
            )
            gate_col[i, s * POS : (s + 1) * POS, :] = jnp.broadcast_to(weight, (POS, 128))
        return carry

    lax.fori_loop(0, PLANES, build_plane, 0)

    def gather(k, source):
        dc = CHUNKS[k][1]
        picked = jnp.dot(onehot[source], tok[k][source], preferred_element_type=F32)
        for part in range(dc // 128):
            lanes = slice(part * 128, (part + 1) * 128)
            scaled = (picked[:, lanes] * gate_col[source]).astype(BF16)
            scaled = scaled.reshape(PEERS, 2, POS, 128)
            rows_out[k % 2, :, :, source, :, lanes] = scaled

    def rows_copy(k, to, index):
        dc = CHUNKS[k][1]
        return remote(
            rows_out.at[k % 2, to, :, :, :, pl.ds(0, dc)],
            rows_in[k].at[:, p],
            sem_rows,
            (k, index),
            (k, index),
            dev_p(to),
        )

    def rows_arrival(k, source, index):
        view = rows_in[k].at[:, source]
        return remote(view, view, sem_rows, (k, index), (k, index), dev_p(source))

    def own(src, dst, stage, k):
        return pltpu.make_async_copy(src, dst, sem_own.at[stage, k])

    def rows_own(k):
        dc = CHUNKS[k][1]
        return own(rows_out.at[k % 2, p, :, :, :, pl.ds(0, dc)], rows_in[k].at[:, p], 0, k)

    def rows_sent(k):
        others(lambda i: rows_copy(k, peer(i), i).wait_send())

    def stage_ring(k):
        own_tok[k].wait()
        if k >= 2:
            rows_sent(k - 2)
        gather(k, z)
        for step in (1, 2, 3, 4):
            for way, half in ring_parts(step):
                ring_arrival(k, way, step, half).wait_recv()
                if step < 3 or (step == 3 and half == way):
                    ring_send(k, way, step + 1, half).start()
            if step == 1 and k + 1 < N:
                ring_begin(k + 1)
            gather(k, plane(step))
            if step < 4:
                gather(k, plane(-step))
        rows_own(k).start()
        others(lambda i: rows_copy(k, peer(i), i).start())

    def part_view(k, to):
        return part_out.at[k % 2, to, :, :, :, pl.ds(0, CHUNKS[k][1])]

    def part_copy(k, to, index):
        return remote(
            part_view(k, to), relay_x[k].at[:, p], sem_px, (k, index), (k, index), dev_p(to)
        )

    def part_arrival(k, source, index):
        view = relay_x[k].at[:, source]
        return remote(view, view, sem_px, (k, index), (k, index), dev_p(source))

    def part_own(k):
        return own(part_view(k, p), relay_x[k].at[:, p], 1, k)

    def stage_matmul(k):
        dc = CHUNKS[k][1]
        rows_own(k).wait()
        others(lambda i: rows_arrival(k, peer(-i), i).wait_recv())
        if k >= 2:
            others(lambda i: part_copy(k - 2, peer(i), i).wait_send())

        def block(i, carry):
            w = lax.rem(i, 2)
            part = lax.rem(y + i // 2, 4)
            total = jnp.zeros((FPART, dc), F32)
            for q in range(PEERS):
                total += jnp.dot(
                    hid_t[w, part, q],
                    rows_in[k][w, q].reshape(PLANES * POS, dc),
                    preferred_element_type=F32,
                )
            rounded = total.astype(BF16).reshape(2, PEERS, ROWS, dc)
            for h in range(2):
                for q in range(PEERS):
                    part_out[k % 2, q, w, 2 * part + h, :, 0:dc] = rounded[h, q]
            return carry

        lax.fori_loop(0, 8, block, 0)
        part_own(k).start()
        others(lambda i: part_copy(k, peer(i), i).start())

    def grad_copy(k, to, index):
        return remote(
            relay_x[k].at[:, :, to],
            grad_in[k].at[:, z],
            sem_pz,
            (k, index),
            (k, index),
            dev_z(to),
        )

    def grad_arrival(k, source, index):
        view = grad_in[k].at[:, source]
        return remote(view, view, sem_pz, (k, index), (k, index), dev_z(source))

    def grad_own(k):
        return own(relay_x[k].at[:, :, z], grad_in[k].at[:, z], 2, k)

    def stage_forward(k):
        part_own(k).wait()
        others(lambda i: part_arrival(k, peer(-i), i).wait_recv())
        others(lambda i: grad_copy(k, plane(i), i).start())
        grad_own(k).start()

    def step_view(k, to):
        return step_out.at[k % 2, :, to, :, :, pl.ds(0, CHUNKS[k][1])]

    def step_copy(k, to, index):
        return remote(
            step_view(k, to), relay_s[k].at[:, z], sem_sz, (k, index), (k, index), dev_z(to)
        )

    def step_arrival(k, source, index):
        view = relay_s[k].at[:, source]
        return remote(view, view, sem_sz, (k, index), (k, index), dev_z(source))

    def step_own(k):
        return own(step_view(k, z), relay_s[k].at[:, z], 3, k)

    tile = 256
    per_tile = tile // (PEERS * ROWS)

    def stage_adam(k):
        dc = CHUNKS[k][1]
        grad_own(k).wait()
        others(lambda i: grad_arrival(k, plane(-i), i).wait_recv())
        if k >= 2:
            others(lambda i: step_copy(k - 2, plane(i), i).wait_send())
        for copy in load_moments(k):
            copy.wait()

        def block(i, carry):
            rows = pl.ds(pl.multiple_of(i * tile, tile), tile)
            planes = pl.ds(i * per_tile, per_tile)
            twins = grad_in[k][1].reshape(PLANES * PEERS * ROWS, dc)
            gradient = grad_in[k][0, planes].reshape(tile, dc).astype(F32)
            gradient += jnp.dot(kron[rows, :], twins, preferred_element_type=F32)
            first = beta_first * mom[k % 2, 0, rows, 0:dc].astype(F32)
            first += (1.0 - beta_first) * gradient
            second = beta_second * mom[k % 2, 1, rows, 0:dc].astype(F32)
            second += (1.0 - beta_second) * gradient * gradient
            value = first / bias_first / (jnp.sqrt(second / bias_second) + adam_eps)
            value = value.astype(BF16).reshape(per_tile, PEERS, ROWS, dc)
            step_out[k % 2, 0, planes, :, :, 0:dc] = value
            return carry

        lax.fori_loop(0, PLANES // per_tile, block, 0)

        def twin(i, carry):
            rows = pl.ds(pl.multiple_of(i * tile, tile), tile)
            planes = pl.ds(i * per_tile, per_tile)
            steps = step_out[k % 2, 0, :, :, :, 0:dc].reshape(PLANES * PEERS * ROWS, dc)
            value = jnp.dot(kron_t[rows, :], steps, preferred_element_type=F32)
            value = value.astype(BF16).reshape(per_tile, PEERS, ROWS, dc)
            step_out[k % 2, 1, planes, :, :, 0:dc] = value
            return carry

        lax.fori_loop(0, PLANES // per_tile, twin, 0)
        step_own(k).start()
        others(lambda i: step_copy(k, plane(i), i).start())
        if k + 2 < N:
            for copy in load_moments(k + 2):
                copy.start()

    def out_view(k, source):
        return out.at[:, :, source, :, pl.ds(CHUNKS[k][0], CHUNKS[k][1])]

    def out_copy(k, to, index):
        return remote(
            relay_s[k].at[:, :, to], out_view(k, p), sem_sx, (k, index), (k, index), dev_p(to)
        )

    def out_arrival(k, source, index):
        view = out_view(k, source)
        return remote(view, view, sem_sx, (k, index), (k, index), dev_p(source))

    def out_own(k):
        return own(relay_s[k].at[:, :, p], out_view(k, p), 4, k)

    def stage_return(k):
        step_own(k).wait()
        others(lambda i: step_arrival(k, plane(-i), i).wait_recv())
        out_own(k).start()
        others(lambda i: out_copy(k, peer(i), i).start())

    def build_kron():
        target = trow[...]
        for i in range(PLANES):
            rows = lax.broadcasted_iota(jnp.int32, (128, 1024), 0) + i * 128
            kron[i * 128 : (i + 1) * 128, :] = (
                jnp.where(rows == target, 1.0, 0.0).astype(BF16)
            )
            column = jnp.broadcast_to(target[:, i * 128 : (i + 1) * 128].astype(F32), (128, 128)).T
            for j in range(PLANES):
                lanes = lax.broadcasted_iota(jnp.int32, (128, 128), 1) + j * 128
                kron_t[i * 128 : (i + 1) * 128, j * 128 : (j + 1) * 128] = jnp.where(
                    lanes.astype(F32) == column, 1.0, 0.0
                ).astype(BF16)

    hid_second = [(4, 0, y_part(-1), 1), (5, 1, y_part(1), -1)]

    def forward_hidden():
        hid_copy(0, 0, y_part(-1), 1).wait_recv()
        hid_copy(4, 0, y_part(-1), 1).start()
        hid_copy(3, 1, y_part(1), -1).wait_recv()
        hid_copy(5, 1, y_part(1), -1).start()

    def finish_hidden():
        hid_copy(1, 1, y_part(-1), 1).wait_recv()
        hid_copy(2, 0, y_part(1), -1).wait_recv()
        hid_copy(4, 0, y_part(2), 1).wait_recv()
        hid_copy(5, 1, y_part(2), -1).wait_recv()

    stage_ring(0)
    forward_hidden()
    build_kron()
    stage_ring(1)
    finish_hidden()
    stage_matmul(0)
    stage_ring(2)
    stage_forward(0)
    stage_matmul(1)
    stage_ring(3)
    stage_forward(1)
    stage_matmul(2)
    stage_adam(0)
    stage_forward(2)
    stage_matmul(3)
    stage_adam(1)
    stage_return(0)
    stage_forward(3)
    stage_adam(2)
    stage_return(1)
    stage_adam(3)
    stage_return(2)
    stage_return(3)

    others(lambda i: meta_copy(i).wait_send())
    for index, w, d in hid_first:
        hid_copy(index, w, y, d).wait_send()
    for index, w, part, d in hid_second:
        hid_copy(index, w, part, d).wait_send()
    for k in range(N):
        for step in (1, 2, 3, 4):
            for way, half in ring_parts(step):
                ring_send(k, way, step, half).wait_send()
        others(lambda i: grad_copy(k, plane(i), i).wait_send())
        others(lambda i: out_copy(k, peer(i), i).wait_send())
        if k >= N - 2:
            rows_sent(k)
            others(lambda i: part_copy(k, peer(i), i).wait_send())
            others(lambda i: step_copy(k, plane(i), i).wait_send())
        others(lambda i: out_arrival(k, peer(-i), i).wait_recv())
        out_own(k).wait()


def expert_steps(og, meta, hid, trow, m1, m2):
    anywhere = pl.BlockSpec(memory_space=pl.ANY)
    relays = [
        jax.ShapeDtypeStruct((2, PEERS, PLANES, ROWS, dc), BF16) for _, dc in CHUNKS
    ]
    returns = [
        jax.ShapeDtypeStruct((2, PLANES, PEERS, ROWS, dc), BF16) for _, dc in CHUNKS
    ]
    shape = jax.ShapeDtypeStruct((2, PLANES, PEERS, ROWS, WIDTH), BF16)
    widest = max(dc for _, dc in CHUNKS)
    dma = pltpu.SemaphoreType.DMA
    scratch = [pltpu.VMEM((PLANES, TOKENS, dc), BF16) for _, dc in CHUNKS]
    scratch += [pltpu.VMEM((2, PEERS, PLANES, POS, dc), BF16) for _, dc in CHUNKS]
    scratch += [pltpu.VMEM((2, PLANES, PEERS, ROWS, dc), BF16) for _, dc in CHUNKS]
    scratch += [
        pltpu.VMEM((PLANES, 8, TOKENS), F32),
        pltpu.VMEM((PLANES, 16 * POS, TOKENS), BF16),
        pltpu.VMEM((PLANES, 16 * POS, 128), F32),
        pltpu.VMEM((2, PEERS, 2, PLANES, POS, widest), BF16),
        pltpu.VMEM((2, 4, PEERS, FPART, PLANES * POS), BF16),
        pltpu.VMEM((2, PEERS, 2, PLANES, ROWS, widest), BF16),
        pltpu.VMEM((2, 2, PLANES, PEERS, ROWS, widest), BF16),
        pltpu.VMEM((2, 2, PLANES * PEERS * ROWS, widest), BF16),
        pltpu.VMEM((1024, 1024), BF16),
        pltpu.VMEM((1024, 1024), BF16),
        dma((2, 8)),
        dma((2, N, 2, 4, 2)),
        dma((2, 6)),
        dma((2, N, 8)),
        dma((2, N, 8)),
        dma((2, N, 8)),
        dma((2, N, 8)),
        dma((2, N, 8)),
        dma((N + 6,)),
        dma((5, N)),
    ]
    results = pl.pallas_call(
        kernel,
        out_shape=[shape] + relays + returns,
        in_specs=[anywhere, anywhere, anywhere, pl.BlockSpec(memory_space=pltpu.VMEM), anywhere, anywhere],
        out_specs=[anywhere] * (1 + 2 * N),
        scratch_shapes=scratch,
        compiler_params=pltpu.CompilerParams(
            collective_id=0, has_side_effects=True, vmem_limit_bytes=62 * 1024 * 1024
        ),
        cost_estimate=pl.CostEstimate(
            flops=50_000_000_000, bytes_accessed=60_000_000, transcendentals=2_000_000
        ),
    )(og, meta, hid, trow, m1, m2)
    return results[0]


def shards(out_grad, routes, gates, dup_owner, hidden, moment1, moment2, value_grad, value_proj):
    experts = PLANES * PEERS
    meta = jnp.concatenate([routes.astype(F32), gates], axis=1).T
    hid = hidden[0].reshape(PLANES, PEERS, 2, hidden.shape[3], FPART)
    hid = jnp.pad(
        hid.transpose(1, 2, 0, 3, 4), ((0, 0), (0, 0), (0, 0), (0, POS - hidden.shape[3]), (0, 0))
    )
    trow = (dup_owner[:, None] * ROWS + jnp.arange(ROWS, dtype=jnp.int32)[None, :]).reshape(1, -1)
    steps = expert_steps(
        out_grad,
        meta,
        hid,
        trow,
        moment1.reshape(experts * ROWS, WIDTH),
        moment2.reshape(experts * ROWS, WIDTH),
    )
    latent_grad = lax.psum_scatter(
        lax.dot_general(
            value_proj, value_grad, (((1,), (1,)), ((), ())), preferred_element_type=F32
        ),
        "dp",
        scatter_dimension=0,
        tiled=True,
    ).astype(BF16)
    return (steps.reshape(1, 2, PLANES * PEERS * ROWS, WIDTH), latent_grad)


def solution(mesh):
    in_specs = (
        P("expert", "dp"),
        P("expert", None),
        P("expert", None),
        P(),
        P("expert", None, None, None, "dp"),
        P(None, "expert", "dp"),
        P(None, "expert", "dp"),
        P("expert", "dp"),
        P(None, "dp"),
    )
    out_specs = (P("expert", None, None, "dp"), P("dp", "expert"))
    return jax.shard_map(shards, mesh=mesh, in_specs=in_specs, out_specs=out_specs, check_vma=False)
```

time: 581 us -> 354 us (0.61)
  waiting for transfers between devices: 389 us -> 0.04 us
  Pallas kernels: 0 us -> 321 us
  local copies, waits for them, and re-layouts: 95.9 us -> 9.75 us
  starting transfers between devices: 32.2 us -> 0.04 us
  other arithmetic: 27.1 us -> 2.35 us
  matrix products: 20.9 us -> 3.32 us
    all_to_all x3 -> x0, waiting for transfers between devices: 361 us -> none  [the longest x1 160 us: shards(): lax.all_to_all(partial_value, 'expert', split_axis=1, concat_axis=1, tile...]
    pallas_call x0 -> x1, Pallas kernels: none -> 321 us  [expert_steps(): pl.pallas_call(kernel, out_shape=[shape] + relays + returns, in_specs=[an...]
    all_to_all x3 -> x0, starting transfers between devices: 32.1 us -> none  [the longest x1 13.3 us: shards(): lax.all_to_all(outgoing, 'expert', split_axis=0, concat_axis=0, tiled=True)]
    reduce_scatter x1, waiting for transfers between devices: 28.3 us -> 0.02 us  [shards(): lax.psum_scatter(lax.dot_general(value_proj, value_grad, (((1,), (1,)), (...]
    slice x2 -> x0, local copies, waits for them, and re-layouts: 23 us -> none  [the longest x1 14.8 us: one_slot(): arrived[:, slot_index]]
    reshape x2 -> x0, local copies, waits for them, and re-layouts: 21.3 us -> none  [shards(): outgoing = outgoing.reshape(groups, 2, capacity, width_part)]
    dot_general x3 -> x0, matrix products: 18.8 us -> none  [the longest x2 12.2 us: one_slot(): jnp.einsum('scf,scd->fd', piece_slot, arrived[:, slot_index], preferred_e...]
    scatter x1 -> x0, other arithmetic: 17.7 us -> none  [shards(): jnp.zeros((slot_total * capacity, width_part), jnp.bfloat16).at[target]]
  transfers between devices with their start and end apart: 5 -> 1, of which waited for: 4 -> 0; matrix products, arithmetic and copies ran while one was open for 3% -> 1% of each run, Pallas kernels for 0% -> 92%
where the time goes in v1:
time: 354 us; the launch traced here: 350 us
  Pallas kernels  321 us (91%)
  between operations  14.1 us (4%)
  local copies, waits for them, and re-layouts  9.75 us (3%)
    pallas_call x1, Pallas kernels, expert_steps(): pl.pallas_call(kernel, out_shape=[shape] + relays + returns, in_specs=[an...  321 us
  transfers between devices with their start and end apart: 1, of which 0 were waited for; matrix products, arithmetic and copies ran while one was open for 1% of the time, Pallas kernels for 92%

profile of v1, /device:TPU:1, one launch (start us, length us, event | category | flops | bytes accessed | tf_op | source)
XLA Modules:
  0.0 350.3 jit_solution(7940078106738929930)
XLA Ops:
  7.2 0.0 copy-start
  7.2 0.0 reduce-scatter.2.cloned.1.call-start
  7.2 1.3 copy-done
  8.5 3.3 fusion
  11.8 0.0 reduce-scatter.2.cloned.1.call-update
  11.8 0.0 copy-start.3
  11.8 0.0 copy-start.2
  11.9 1.9 copy.16
  13.8 0.0 copy-done.3
  13.8 0.1 iota_add_fusion
  13.9 0.7 add.30.trow
  14.6 0.0 copy-done.2
  14.6 0.0 copy-start.1
  14.6 1.7 pad.4.hid
  16.3 0.0 copy-done.1
  16.3 0.6 maximum_bitcast_fusion.meta
  16.9 320.7 %shard_map.104 = (bf16[2,8,8,16,896]{4,3,2,1,0:T(8,128)(2,1)}, bf16[2,8,8,16,256]{4,3,2,1,0:T(8,128)(2,1)}, bf16[2,8,8,16,256]{4,3,2,1,0:T(8,128)(2,1)}, bf16[2,...) custom-call(bf16[640,896]{1,0:T(8,128)(2,1)} %og.1, ...), custom_call_target="tpu_custom_call" | custom-call | flops 49999998976 | bytes 60000000 | tf_op jit(solution)/shard_map/pallas_call | solution.py:534
  337.6 0.0 reduce-scatter.2.cloned.1.call-done
  337.6 1.7 convert_element_type.9
  339.3 4.2 %copy.18 = bf16[1,2,1024,896]{3,2,1,0:T(8,128)(2,1)} copy(bf16[1,2,1024,896]{3,2,1,0:T(8,128)(2,1)} %bitcast.12) | data formatting | bytes 7340032
  (2 shorter events, 0.0 us)
Async XLA Ops:
  7.2 1.3 copy-start
  7.2 330.4 %reduce-scatter.2.cloned.1.call-start = ((), (), s32[]{:S(2)}) async-start(), calls=%async_computation.1 | async-start | bytes 1638400 | tf_op jit(solution)/shard_map/reduce_scatter | solution.py:566
  11.8 2.0 copy-start.3
  11.8 2.7 copy-start.2
  14.6 1.7 copy-start.1
Sparse Core Ops, SparseCore 0:
  12.0 39.5 reduce-scatter.1

commit v2 on v1

v2 whole, which is shorter than its diff:
```python
import functools

import jax
import jax.numpy as jnp
from jax import lax
from jax.experimental import pallas as pl
from jax.experimental.pallas import tpu as pltpu
from jax.sharding import PartitionSpec as P

beta_first = 0.9
beta_second = 0.95
adam_eps = 1e-08
bias_first = 1.0 - 0.9**50 * 0.9**50
bias_second = 1.0 - 0.95**50 * 0.95**50

PLANES = 8
PEERS = 8
ROWS = 16
POS = 32
TOKENS = 640
FPART = 256
WIDTH = 896
CHUNKS = ((0, 256), (256, 256), (512, 256), (768, 128))
N = len(CHUNKS)
ORDER = (0, 1, -1, 2, -2, 3, -3, 4)
GROUPS = ((0, 3), (3, 5), (5, 8))
HALF = TOKENS // 2
TURNS = (1, 7, 2, 6, 3, 5, 4)
MESH = pl.DeviceIdType.MESH
F32 = jnp.float32
BF16 = jnp.bfloat16


def kernel(
    og,
    routes,
    gates,
    hid,
    dup,
    m1,
    m2,
    vgrad,
    vproj,
    out,
    latent,
    *refs,
):
    relay_x, relay_s, refs = refs[:N], refs[N : 2 * N], refs[2 * N :]
    tok, refs = refs[:N], refs[N:]
    rows_in, refs = refs[:N], refs[N:]
    grad_in, refs = refs[:N], refs[N:]
    rows_out, refs = refs[:N], refs[N:]
    (
        metas,
        gate_rows,
        onehot,
        gate_col,
        hid_t,
        part_out,
        step_out,
        mom,
        kron,
        kron_t,
        earlier,
        vg,
        vp,
        lat_part,
        lat_in,
        sem_meta,
        sem_ring,
        sem_ring_sent,
        sem_hid,
        sem_rows,
        sem_px,
        sem_pz,
        sem_sz,
        sem_last,
        sem_sx,
        sem_lat,
        sem_local,
        sem_own,
    ) = refs
    me = lax.axis_index("expert")
    y = lax.axis_index("dp")
    z = me // PEERS
    p = me % PEERS

    def plane(d):
        return lax.rem(z + d + PLANES, PLANES)

    def peer(d):
        return lax.rem(p + d + PEERS, PEERS)

    def dev_z(to):
        return {"expert": to * PEERS + p}

    def dev_p(to):
        return {"expert": z * PEERS + to}

    def dev_y(d):
        return {"dp": lax.rem(y + d + 4, 4)}

    def remote(src, dst, sent, arrived, device):
        return pltpu.make_async_remote_copy(
            src_ref=src,
            dst_ref=dst,
            send_sem=sent,
            recv_sem=arrived,
            device_id=device,
            device_id_type=MESH,
        )

    def all_sent(view, sem):
        remote(view, view, sem, sem, dev_p(p)).wait_send()

    def all_arrived(view, sem):
        remote(view, view, sem, sem, dev_p(p)).wait_recv()

    def others(body):
        def step(i, carry):
            body(i)
            return carry

        lax.fori_loop(1, 8, step, 0)

    def planes_in_turn(body):
        for i in TURNS:
            body(i)

    barrier = pltpu.get_barrier_semaphore()

    def greet(i):
        pl.semaphore_signal(barrier, inc=1, device_id=dev_z(plane(i)), device_id_type=MESH)
        pl.semaphore_signal(barrier, inc=1, device_id=dev_p(peer(i)), device_id_type=MESH)

    others(greet)
    for d in (1, 2, 3):
        pl.semaphore_signal(barrier, inc=1, device_id=dev_y(d), device_id_type=MESH)

    def local(src, dst, index):
        return pltpu.make_async_copy(src, dst, sem_local.at[index])

    own_tok = [
        local(og.at[:, pl.ds(CHUNKS[k][0], CHUNKS[k][1])], tok[k].at[z], k) for k in range(N)
    ]
    load_hid = [
        local(hid.at[plane(d)], rows_out[1].at[:, :, i], N + 6) for i, d in enumerate(ORDER)
    ]
    load_latent = [local(vgrad, vg, N), local(vproj, vp, N + 7)]
    load_meta = [local(routes, metas.at[z], N + 1), local(gates, gate_rows.at[z], N + 8)]

    def load_moments(k):
        c0, dc = CHUNKS[k]
        return [
            local(
                m.at[:, pl.ds(c0, dc)],
                mom.at[k % 2, i, :, pl.ds(0, dc)],
                N + 2 + 2 * (k % 2) + i,
            )
            for i, m in enumerate((m1, m2))
        ]

    for copy in load_hid + load_meta + own_tok[:1]:
        copy.start()

    with jax.named_scope("barrier"):
        pl.semaphore_wait(barrier, 17)

    def meta_copies(i):
        return [
            remote(source, into.at[z], sem_meta.at[0, j], sem_meta.at[1, j], dev_z(plane(i)))
            for j, (source, into) in enumerate(((routes, metas), (gates, gate_rows)))
        ]

    def send_meta(i):
        for copy in meta_copies(i):
            copy.start()

    def late_loads():
        for copy in own_tok[1:] + load_latent:
            copy.start()
        for k in (0, 1):
            for copy in load_moments(k):
                copy.start()

    def ring_send(k, way, step, half):
        c0, dc = CHUNKS[k]
        sign = 1 - 2 * way
        block = plane(-sign * (step - 1))
        rows = pl.ds(half * HALF, HALF)
        source = og.at[rows, pl.ds(c0, dc)] if step == 1 else tok[k].at[block, rows]
        arrived = sem_ring.at[k, way, step - 1, half]
        return remote(
            source, tok[k].at[block, rows], sem_ring_sent.at[k], arrived, dev_z(plane(sign))
        )

    def ring_arrival(k, way, step, half):
        sign = 1 - 2 * way
        block = plane(-sign * step)
        rows = pl.ds(half * HALF, HALF)
        arrived = sem_ring.at[k, way, step - 1, half]
        view = tok[k].at[block, rows]
        return remote(view, view, sem_ring_sent.at[k], arrived, dev_z(plane(sign)))

    def ring_parts(step):
        return [(way, half) for half in (0, 1) for way in (0, 1) if step < 4 or half == way]

    def ring_begin(k):
        for way, half in ring_parts(1):
            ring_send(k, way, 1, half).start()

    def ring_forward(k, step):
        for way, half in ring_parts(step):
            ring_arrival(k, way, step, half).wait_recv()
            if step < 3 or (step == 3 and half == way):
                ring_send(k, way, step + 1, half).start()

    def transpose_half(w):
        def piece(q, carry):
            hid_t[w, y, q] = rows_out[1][q, w].reshape(PLANES * POS, FPART).T
            return carry

        lax.fori_loop(0, PEERS, piece, 0)

    def y_part(d):
        return lax.rem(y + d + 4, 4)

    def hid_copy(index, w, part, d):
        view = hid_t.at[w, y_part(part)]
        return remote(view, view, sem_hid.at[6], sem_hid.at[index], dev_y(d))

    hid_copies = ((0, 0, 0, 1), (1, 1, 0, -1), (2, 1, 0, 1), (3, 0, 0, -1), (4, 0, -1, 1), (5, 1, 1, -1))

    def hid_send(index):
        hid_copy(*hid_copies[index]).start()

    def hid_wait(index):
        number, w, part, d = hid_copies[index]
        hid_copy(number, w, part - d, d).wait_recv()

    def build_plane(i):
        slot_of = lax.broadcasted_iota(jnp.int32, (16, TOKENS), 0) + z * 16
        named = jnp.zeros((16, TOKENS), F32)
        gate = jnp.zeros((16, TOKENS), F32)
        for k in range(4):
            match = slot_of == metas[i, k : k + 1, :]
            named = jnp.where(match, 1.0, named)
            gate = jnp.where(match, gate_rows[i, k : k + 1, :], gate)
        rank = jnp.dot(named.astype(BF16), earlier[...], preferred_element_type=F32)
        rank = jnp.where(named > 0.5, rank, -1.0)
        position = lax.broadcasted_iota(jnp.int32, (POS, TOKENS), 0).astype(F32)
        for s in range(16):
            chosen = position == rank[s : s + 1, :]
            onehot[i, s * POS : (s + 1) * POS, :] = jnp.where(chosen, 1.0, 0.0).astype(BF16)
            weight = jnp.sum(
                jnp.where(chosen, gate[s : s + 1, :], 0.0), axis=1, keepdims=True
            )
            gate_col[i, s * POS : (s + 1) * POS, :] = jnp.broadcast_to(weight, (POS, 128))

    def build(*distances):
        for d in distances:
            build_plane(plane(d))

    def gather(k, d):
        dc = CHUNKS[k][1]
        source, place = plane(d), ORDER.index(d)
        picked = jnp.dot(onehot[source], tok[k][source], preferred_element_type=F32)
        for part in range(dc // 128):
            lanes = slice(part * 128, (part + 1) * 128)
            scaled = (picked[:, lanes] * gate_col[source]).astype(BF16)
            rows_out[k][:, :, place, :, lanes] = scaled.reshape(PEERS, 2, POS, 128)

    def rows_copy(k, group, to):
        low, high = GROUPS[group]
        return remote(
            rows_out[k].at[to, :, low:high],
            rows_in[k].at[:, p, low:high],
            sem_rows.at[0, k],
            sem_rows.at[1, k],
            dev_p(to),
        )

    def own(src, dst, stage, k):
        return pltpu.make_async_copy(src, dst, sem_own.at[stage, k])

    def rows_own(k):
        return own(rows_out[k].at[p], rows_in[k].at[:, p], 0, k)

    def pick(k, *distances):
        for d in distances:
            gather(k, d)

    def send_rows(k, group):
        others(lambda i: rows_copy(k, group, peer(i)).start())
        if group == len(GROUPS) - 1:
            rows_own(k).start()

    def lat_copy(d):
        return remote(
            lat_part.at[y_part(d)], lat_in.at[d - 1], sem_lat.at[0], sem_lat.at[1], dev_y(d)
        )

    def latent_begin():
        for copy in load_latent:
            copy.wait()
        for i in range(4):
            lat_part[i] = lax.dot_general(
                vp[i * 128 : (i + 1) * 128, :],
                vg[...],
                (((1,), (1,)), ((), ())),
                preferred_element_type=F32,
            )
        for d in (1, 2, 3):
            lat_copy(d).start()

    def latent_end():
        all_arrived(lat_in, sem_lat.at[1])
        total = lat_part[y] + lat_in[0] + lat_in[1] + lat_in[2]
        vp[0:128, 0:TOKENS] = total.astype(BF16)
        store = local(vp.at[pl.ds(0, 128), pl.ds(0, TOKENS)], latent, N + 7)
        store.start()
        store.wait()

    def part_view(k, to):
        return part_out.at[k % 2, to, :, :, :, pl.ds(0, CHUNKS[k][1])]

    def part_copy(k, to):
        return remote(
            part_view(k, to), relay_x[k].at[:, p], sem_px.at[0, k], sem_px.at[1, k], dev_p(to)
        )

    def part_sent(k):
        all_sent(part_out.at[k % 2, 0:7, :, :, :, pl.ds(0, CHUNKS[k][1])], sem_px.at[0, k])

    def part_own(k):
        return own(part_view(k, p), relay_x[k].at[:, p], 1, k)

    def stage_matmul(k):
        dc = CHUNKS[k][1]
        rows_own(k).wait()
        all_arrived(rows_in[k].at[:, 0:7], sem_rows.at[1, k])
        if k >= 2:
            part_sent(k - 2)

        def block(i, carry):
            w = lax.rem(i, 2)
            part = lax.rem(y + i // 2, 4)
            total = jnp.zeros((FPART, dc), F32)
            for q in range(PEERS):
                total += jnp.dot(
                    hid_t[w, part, q],
                    rows_in[k][w, q].reshape(PLANES * POS, dc),
                    preferred_element_type=F32,
                )
            rounded = total.astype(BF16).reshape(2, PEERS, ROWS, dc)
            for h in range(2):
                for q in range(PEERS):
                    part_out[k % 2, q, w, 2 * part + h, :, 0:dc] = rounded[h, q]
            return carry

        lax.fori_loop(0, 8, block, 0)
        part_own(k).start()
        others(lambda i: part_copy(k, peer(i)).start())

    def grad_copy(k, to):
        return remote(
            relay_x[k].at[:, :, to],
            grad_in[k].at[:, z],
            sem_pz.at[0, k],
            sem_pz.at[1, k],
            dev_z(to),
        )

    def grad_own(k):
        return own(relay_x[k].at[:, :, z], grad_in[k].at[:, z], 2, k)

    def stage_forward(k):
        part_own(k).wait()
        all_arrived(relay_x[k].at[:, 0:7], sem_px.at[1, k])
        planes_in_turn(lambda i: grad_copy(k, plane(i)).start())
        grad_own(k).start()

    def step_view(k, to):
        return step_out.at[k % 2, :, to, :, :, pl.ds(0, CHUNKS[k][1])]

    def step_copy(k, to, index):
        arrived = sem_sz.at[1, k] if k < N - 2 else sem_last.at[k - (N - 2), index]
        return remote(step_view(k, to), relay_s[k].at[:, z], sem_sz.at[0, k], arrived, dev_z(to))

    def step_sent(k):
        all_sent(step_out.at[k % 2, :, 0:7, :, :, pl.ds(0, CHUNKS[k][1])], sem_sz.at[0, k])

    def step_own(k):
        return own(step_view(k, z), relay_s[k].at[:, z], 3, k)

    tile = 256
    per_tile = tile // (PEERS * ROWS)

    def stage_adam(k):
        dc = CHUNKS[k][1]
        grad_own(k).wait()
        all_arrived(grad_in[k].at[:, 0:7], sem_pz.at[1, k])
        if k >= 2:
            step_sent(k - 2)
        for copy in load_moments(k):
            copy.wait()

        def block(i, carry):
            rows = pl.ds(pl.multiple_of(i * tile, tile), tile)
            planes = pl.ds(i * per_tile, per_tile)
            twins = grad_in[k][1].reshape(PLANES * PEERS * ROWS, dc)
            gradient = grad_in[k][0, planes].reshape(tile, dc).astype(F32)
            gradient += jnp.dot(kron[rows, :], twins, preferred_element_type=F32)
            first = beta_first * mom[k % 2, 0, rows, 0:dc].astype(F32)
            first += (1.0 - beta_first) * gradient
            second = beta_second * mom[k % 2, 1, rows, 0:dc].astype(F32)
            second += (1.0 - beta_second) * gradient * gradient
            value = first / bias_first / (jnp.sqrt(second / bias_second) + adam_eps)
            value = value.astype(BF16).reshape(per_tile, PEERS, ROWS, dc)
            step_out[k % 2, 0, planes, :, :, 0:dc] = value
            return carry

        lax.fori_loop(0, PLANES // per_tile, block, 0)

        def twin(i, carry):
            rows = pl.ds(pl.multiple_of(i * tile, tile), tile)
            planes = pl.ds(i * per_tile, per_tile)
            steps = step_out[k % 2, 0, :, :, :, 0:dc].reshape(PLANES * PEERS * ROWS, dc)
            value = jnp.dot(kron_t[rows, :], steps, preferred_element_type=F32)
            value = value.astype(BF16).reshape(per_tile, PEERS, ROWS, dc)
            step_out[k % 2, 1, planes, :, :, 0:dc] = value
            return carry

        lax.fori_loop(0, PLANES // per_tile, twin, 0)
        step_own(k).start()
        planes_in_turn(lambda i: step_copy(k, plane(i), i).start())
        if k + 2 < N:
            for copy in load_moments(k + 2):
                copy.start()

    def columns(k):
        return pl.ds(CHUNKS[k][0], CHUNKS[k][1])

    def out_copy(k, to):
        return remote(
            relay_s[k].at[:, :, to],
            out.at[:, :, p, :, columns(k)],
            sem_sx.at[0, k],
            sem_sx.at[1, k],
            dev_p(to),
        )

    def out_own(k):
        return own(relay_s[k].at[:, :, p], out.at[:, :, p, :, columns(k)], 4, k)

    def plane_copy(k, source, to):
        return remote(
            relay_s[k].at[:, source, to],
            out.at[:, source, p, :, columns(k)],
            sem_sx.at[0, k],
            sem_sx.at[1, k],
            dev_p(to),
        )

    def stage_return(k):
        step_own(k).wait()
        if k < N - 2:
            all_arrived(relay_s[k].at[:, 0:7], sem_sz.at[1, k])
            out_own(k).start()
            others(lambda i: out_copy(k, peer(i)).start())
            return
        others(lambda i: plane_copy(k, z, peer(i)).start())
        for index in TURNS:
            source = plane(-index)
            view = relay_s[k].at[:, source]
            remote(
                view, view, sem_sz.at[0, k], sem_last.at[k - (N - 2), index], dev_z(source)
            ).wait_recv()
            others(lambda i: plane_copy(k, source, peer(i)).start())
        out_own(k).start()

    def drain_start():
        all_sent(metas.at[0:7], sem_meta.at[0, 0])
        all_sent(gate_rows.at[0:7], sem_meta.at[0, 1])
        all_sent(hid_t.at[:, 0:3], sem_hid.at[6])
        all_sent(lat_in, sem_lat.at[0])
        for k in range(N):
            all_sent(tok[k].at[0:7], sem_ring_sent.at[k])
            all_sent(rows_out[k].at[0:7], sem_rows.at[0, k])

    def drain_parts():
        for k in (N - 2, N - 1):
            part_sent(k)
        for k in range(N):
            all_sent(relay_x[k].at[:, :, 0:7], sem_pz.at[0, k])

    def drain_out(k):
        all_sent(relay_s[k].at[:, :, 0:7], sem_sx.at[0, k])
        all_arrived(out.at[:, :, 0:7, :, columns(k)], sem_sx.at[1, k])
        out_own(k).wait()

    def build_kron():
        spread = lax.broadcasted_iota(jnp.int32, (PLANES * PEERS, 1024), 1) // ROWS
        spread = spread == lax.broadcasted_iota(jnp.int32, (PLANES * PEERS, 1024), 0)
        owners = jnp.broadcast_to(dup[...].astype(F32), (16, PLANES * PEERS)).astype(BF16)
        owners = jnp.dot(owners, spread.astype(F32).astype(BF16), preferred_element_type=F32)
        offset = lax.broadcasted_iota(jnp.int32, (1, 1024), 1) % ROWS
        target = owners[0:1, :].astype(jnp.int32) * ROWS + offset
        for i in range(PLANES):
            rows = lax.broadcasted_iota(jnp.int32, (128, 1024), 0) + i * 128
            kron[i * 128 : (i + 1) * 128, :] = (
                jnp.where(rows == target, 1.0, 0.0).astype(BF16)
            )
            column = jnp.broadcast_to(target[:, i * 128 : (i + 1) * 128].astype(F32), (128, 128)).T
            for j in range(PLANES):
                lanes = lax.broadcasted_iota(jnp.int32, (128, 128), 1) + j * 128
                kron_t[i * 128 : (i + 1) * 128, j * 128 : (j + 1) * 128] = jnp.where(
                    lanes.astype(F32) == column, 1.0, 0.0
                ).astype(BF16)

    def wait_hid():
        for copy in load_hid:
            copy.wait()

    def prepare():
        for copy in load_meta:
            copy.wait()
        earlier[...] = (
            lax.broadcasted_iota(jnp.int32, (TOKENS, TOKENS), 0)
            < lax.broadcasted_iota(jnp.int32, (TOKENS, TOKENS), 1)
        ).astype(F32).astype(BF16)

    def meta_arrivals():
        all_arrived(metas.at[0:7], sem_meta.at[1, 0])
        all_arrived(gate_rows.at[0:7], sem_meta.at[1, 1])

    def own_wait(k):
        own_tok[k].wait()

    def hid_pass():
        hid_wait(0)
        hid_send(4)
        hid_send(2)
        hid_wait(1)
        hid_send(5)
        hid_send(3)

    def hid_finish():
        for index in (2, 3, 4, 5):
            hid_wait(index)

    with jax.named_scope("others"):
        others(send_meta)
    with jax.named_scope("ring_begin0"):
        ring_begin(0)
    with jax.named_scope("ring_begin1"):
        ring_begin(1)
    with jax.named_scope("wait_hid"):
        wait_hid()
    with jax.named_scope("transpose_half0"):
        transpose_half(0)
    with jax.named_scope("hid_send0"):
        hid_send(0)
    with jax.named_scope("transpose_half1"):
        transpose_half(1)
    with jax.named_scope("hid_send1"):
        hid_send(1)
    with jax.named_scope("late_loads"):
        late_loads()
    with jax.named_scope("prepare"):
        prepare()
    with jax.named_scope("meta_arrivals"):
        meta_arrivals()
    with jax.named_scope("build0"):
        build(0)
    with jax.named_scope("own_wait0"):
        own_wait(0)
    with jax.named_scope("pick00"):
        pick(0, 0)
    with jax.named_scope("build11"):
        build(1, -1)
    with jax.named_scope("ring_forward01"):
        ring_forward(0, 1)
    with jax.named_scope("pick011"):
        pick(0, 1, -1)
    with jax.named_scope("send_rows00"):
        send_rows(0, 0)
    with jax.named_scope("build22"):
        build(2, -2)
    with jax.named_scope("own_wait1"):
        own_wait(1)
    with jax.named_scope("pick10"):
        pick(1, 0)
    with jax.named_scope("ring_forward11"):
        ring_forward(1, 1)
    with jax.named_scope("pick111"):
        pick(1, 1, -1)
    with jax.named_scope("send_rows10"):
        send_rows(1, 0)
    with jax.named_scope("ring_forward02"):
        ring_forward(0, 2)
    with jax.named_scope("pick022"):
        pick(0, 2, -2)
    with jax.named_scope("send_rows01"):
        send_rows(0, 1)
    with jax.named_scope("build33"):
        build(3, -3)
    with jax.named_scope("hid_pass"):
        hid_pass()
    with jax.named_scope("ring_forward12"):
        ring_forward(1, 2)
    with jax.named_scope("pick122"):
        pick(1, 2, -2)
    with jax.named_scope("send_rows11"):
        send_rows(1, 1)
    with jax.named_scope("build4"):
        build(4)
    with jax.named_scope("build_kron"):
        build_kron()
    with jax.named_scope("ring_forward03"):
        ring_forward(0, 3)
    with jax.named_scope("ring_begin2"):
        ring_begin(2)
    with jax.named_scope("pick033"):
        pick(0, 3, -3)
    with jax.named_scope("ring_forward13"):
        ring_forward(1, 3)
    with jax.named_scope("ring_begin3"):
        ring_begin(3)
    with jax.named_scope("pick133"):
        pick(1, 3, -3)
    with jax.named_scope("ring_forward04"):
        ring_forward(0, 4)
    with jax.named_scope("pick04"):
        pick(0, 4)
    with jax.named_scope("send_rows02"):
        send_rows(0, 2)
    with jax.named_scope("ring_forward21"):
        ring_forward(2, 1)
    with jax.named_scope("own_wait2"):
        own_wait(2)
    with jax.named_scope("pick2011"):
        pick(2, 0, 1, -1)
    with jax.named_scope("send_rows20"):
        send_rows(2, 0)
    with jax.named_scope("ring_forward14"):
        ring_forward(1, 4)
    with jax.named_scope("pick14"):
        pick(1, 4)
    with jax.named_scope("send_rows12"):
        send_rows(1, 2)
    with jax.named_scope("ring_forward31"):
        ring_forward(3, 1)
    with jax.named_scope("own_wait3"):
        own_wait(3)
    with jax.named_scope("pick3011"):
        pick(3, 0, 1, -1)
    with jax.named_scope("ring_forward22"):
        ring_forward(2, 2)
    with jax.named_scope("pick222"):
        pick(2, 2, -2)
    with jax.named_scope("hid_finish"):
        hid_finish()
    with jax.named_scope("matmul0"):
        stage_matmul(0)
    with jax.named_scope("ring_forward32"):
        ring_forward(3, 2)
    with jax.named_scope("pick322"):
        pick(3, 2, -2)
    with jax.named_scope("matmul1"):
        stage_matmul(1)
    with jax.named_scope("ring_forward23"):
        ring_forward(2, 3)
    with jax.named_scope("pick233"):
        pick(2, 3, -3)
    with jax.named_scope("send_rows21"):
        send_rows(2, 1)
    with jax.named_scope("send_rows30"):
        send_rows(3, 0)
    with jax.named_scope("ring_forward33"):
        ring_forward(3, 3)
    with jax.named_scope("pick333"):
        pick(3, 3, -3)
    with jax.named_scope("forward0"):
        stage_forward(0)
    with jax.named_scope("ring_forward24"):
        ring_forward(2, 4)
    with jax.named_scope("pick24"):
        pick(2, 4)
    with jax.named_scope("send_rows22"):
        send_rows(2, 2)
    with jax.named_scope("send_rows31"):
        send_rows(3, 1)
    with jax.named_scope("ring_forward34"):
        ring_forward(3, 4)
    with jax.named_scope("pick34"):
        pick(3, 4)
    with jax.named_scope("send_rows32"):
        send_rows(3, 2)
    with jax.named_scope("forward1"):
        stage_forward(1)
    with jax.named_scope("latent_begin"):
        latent_begin()
    with jax.named_scope("matmul2"):
        stage_matmul(2)
    with jax.named_scope("matmul3"):
        stage_matmul(3)
    with jax.named_scope("adam0"):
        stage_adam(0)
    with jax.named_scope("forward2"):
        stage_forward(2)
    with jax.named_scope("forward3"):
        stage_forward(3)
    with jax.named_scope("adam1"):
        stage_adam(1)
    with jax.named_scope("return0"):
        stage_return(0)
    with jax.named_scope("latent_end"):
        latent_end()
    with jax.named_scope("adam2"):
        stage_adam(2)
    with jax.named_scope("drain_start"):
        drain_start()
    with jax.named_scope("return1"):
        stage_return(1)
    with jax.named_scope("adam3"):
        stage_adam(3)
    with jax.named_scope("drain_parts"):
        drain_parts()
    with jax.named_scope("return2"):
        stage_return(2)
    with jax.named_scope("drain_out0"):
        drain_out(0)
    with jax.named_scope("drain_out1"):
        drain_out(1)
    with jax.named_scope("step_sent2"):
        step_sent(2)
    with jax.named_scope("return3"):
        stage_return(3)
    with jax.named_scope("step_sent3"):
        step_sent(3)
    with jax.named_scope("drain_out2"):
        drain_out(2)
    with jax.named_scope("drain_out3"):
        drain_out(3)


def expert_steps(*operands):
    anywhere = pl.BlockSpec(memory_space=pl.ANY)
    relays = [
        jax.ShapeDtypeStruct((2, PEERS, PLANES, ROWS, dc), BF16) for _, dc in CHUNKS
    ]
    returns = [
        jax.ShapeDtypeStruct((2, PLANES, PEERS, ROWS, dc), BF16) for _, dc in CHUNKS
    ]
    shape = jax.ShapeDtypeStruct((2, PLANES, PEERS, ROWS, WIDTH), BF16)
    widest = max(dc for _, dc in CHUNKS)
    dma = pltpu.SemaphoreType.DMA
    scratch = [pltpu.VMEM((PLANES, TOKENS, dc), BF16) for _, dc in CHUNKS]
    scratch += [pltpu.VMEM((2, PEERS, PLANES, POS, dc), BF16) for _, dc in CHUNKS]
    scratch += [pltpu.VMEM((2, PLANES, PEERS, ROWS, dc), BF16) for _, dc in CHUNKS]
    scratch += [pltpu.VMEM((PEERS, 2, PLANES, POS, dc), BF16) for _, dc in CHUNKS]
    scratch += [
        pltpu.VMEM((PLANES, 4, TOKENS), jnp.int32),
        pltpu.VMEM((PLANES, 4, TOKENS), F32),
        pltpu.VMEM((PLANES, 16 * POS, TOKENS), BF16),
        pltpu.VMEM((PLANES, 16 * POS, 128), F32),
        pltpu.VMEM((2, 4, PEERS, FPART, PLANES * POS), BF16),
        pltpu.VMEM((2, PEERS, 2, PLANES, ROWS, widest), BF16),
        pltpu.VMEM((2, 2, PLANES, PEERS, ROWS, widest), BF16),
        pltpu.VMEM((2, 2, PLANES * PEERS * ROWS, widest), BF16),
        pltpu.VMEM((1024, 1024), BF16),
        pltpu.VMEM((1024, 1024), BF16),
        pltpu.VMEM((TOKENS, TOKENS), BF16),
        pltpu.VMEM((TOKENS, 1024), BF16),
        pltpu.VMEM((512, 1024), BF16),
        pltpu.VMEM((4, 128, TOKENS), F32),
        pltpu.VMEM((3, 128, TOKENS), F32),
        dma((2, 2)),
        dma((N, 2, 4, 2)),
        dma((N,)),
        dma((7,)),
        dma((2, N)),
        dma((2, N)),
        dma((2, N)),
        dma((2, N)),
        dma((2, 8)),
        dma((2, N)),
        dma((2,)),
        dma((N + 9,)),
        dma((5, N)),
    ]
    results = pl.pallas_call(
        kernel,
        out_shape=[shape, jax.ShapeDtypeStruct((128, TOKENS), BF16)] + relays + returns,
        in_specs=[anywhere] * 4 + [pl.BlockSpec(memory_space=pltpu.VMEM)] + [anywhere] * 4,
        out_specs=[anywhere] * (2 + 2 * N),
        scratch_shapes=scratch,
        compiler_params=pltpu.CompilerParams(
            collective_id=0, has_side_effects=True, vmem_limit_bytes=62 * 1024 * 1024
        ),
        cost_estimate=pl.CostEstimate(
            flops=50_000_000_000, bytes_accessed=60_000_000, transcendentals=2_000_000
        ),
    )(*operands)
    return results[0], results[1]


def shards(out_grad, routes, gates, dup_owner, hidden, moment1, moment2, value_grad, value_proj):
    experts = PLANES * PEERS
    hid = jnp.pad(hidden[0], ((0, 0), (0, 0), (0, POS - hidden.shape[3]), (0, 0)))
    hid = hid.reshape(PLANES, PEERS, 2, POS, FPART)
    steps, latent_grad = expert_steps(
        out_grad,
        routes.T,
        gates.T,
        hid,
        dup_owner.reshape(1, -1),
        moment1.reshape(experts * ROWS, WIDTH),
        moment2.reshape(experts * ROWS, WIDTH),
        value_grad,
        value_proj,
    )
    return (steps.reshape(1, 2, PLANES * PEERS * ROWS, WIDTH), latent_grad)


def solution(mesh):
    in_specs = (
        P("expert", "dp"),
        P("expert", None),
        P("expert", None),
        P(),
        P("expert", None, None, None, "dp"),
        P(None, "expert", "dp"),
        P(None, "expert", "dp"),
        P("expert", "dp"),
        P(None, "dp"),
    )
    out_specs = (P("expert", None, None, "dp"), P("dp", "expert"))
    return jax.shard_map(shards, mesh=mesh, in_specs=in_specs, out_specs=out_specs, check_vma=False)
```

time: 354 us -> 278 us (0.79); the launches traced: 350 us -> 278 us
  Pallas kernels: 321 us -> 269 us
  between operations: 14.1 us -> 0.66 us
    pallas_call x1, Pallas kernels: 321 us -> 269 us  [expert_steps(): pl.pallas_call(kernel, out_shape=[shape, jax.ShapeDtypeStruct((128, TOKEN...]
  transfers between devices with their start and end apart: 1 -> 0, of which waited for: 0 -> 0; matrix products, arithmetic and copies ran while one was open for 1% -> 0% of each run, Pallas kernels for 92% -> 0%
where the time goes in v2:
time: 278 us
  Pallas kernels  269 us (97%)
  local copies, waits for them, and re-layouts  8.45 us (3%)
    pallas_call x1, Pallas kernels, expert_steps(): pl.pallas_call(kernel, out_shape=[shape, jax.ShapeDtypeStruct((128, TOKEN...  269 us
    unnamed x5, local copies, waits for them, and re-layouts  6.86 us

profile of v2, /device:TPU:1, one launch (start us, length us, event | category | flops | bytes accessed | tf_op | source)
XLA Modules:
  0.0 278.0 jit_solution(9275160595994202104)
XLA Ops:
  0.6 2.0 copy.12
  2.6 1.6 pad.4.clone
  4.2 268.9 %shard_map.104 = (bf16[2,8,8,16,896]{4,3,2,1,0:T(8,128)(2,1)}, bf16[128,640]{1,0:T(8,128)(2,1)}, bf16[2,8,8,16,256]{4,3,2,1,0:T(8,128)(2,1)}, bf16[2,8,8,16,256]...) custom-call(bf16[640,896]{1,0:T(8,128)(2,1)} %og.1, ...), custom_call_target="tpu_custom_call" | custom-call | flops 49999998976 | bytes 60000000 | tf_op jit(solution)/shard_map/pallas_call | solution.py:793
  273.1 0.0 copy-start
  273.1 4.2 %copy.15 = bf16[1,2,1024,896]{3,2,1,0:T(8,128)(2,1)} copy(bf16[1,2,1024,896]{3,2,1,0:T(8,128)(2,1)} %bitcast.8) | data formatting | bytes 7340032
  277.3 0.0 copy-done
  277.3 0.7 copy.16
Async XLA Ops:
  273.1 4.2 %copy-start = (bf16[128,640]{1,0:T(8,128)(2,1)S(1)}, bf16[128,640]{1,0:T(8,128)(2,1)}, u32[]{:S(2)}) copy-start(bf16[128,640]{1,0:T(8,128)(2,1)} %get-tuple-element.9) | copy-start | bytes 491524

commit v3 on v2

--- a/solution.py
+++ b/solution.py
@@ -16,6 +16,7 @@
 PLANES = 8
 PEERS = 8
 ROWS = 16
+CAP = 30
 POS = 32
 TOKENS = 640
 FPART = 256
@@ -45,11 +46,12 @@
     latent,
     *refs,
 ):
-    relay_x, relay_s, refs = refs[:N], refs[N : 2 * N], refs[2 * N :]
+    relay_x, relay_s, refs = refs[:N], list(refs[N : 2 * N - 2]), refs[2 * N - 2 :]
     tok, refs = refs[:N], refs[N:]
     rows_in, refs = refs[:N], refs[N:]
     grad_in, refs = refs[:N], refs[N:]
     rows_out, refs = refs[:N], refs[N:]
+    relay_s, refs = relay_s + list(refs[:2]), refs[2:]
     (
         metas,
         gate_rows,
@@ -62,6 +64,7 @@
         kron,
         kron_t,
         earlier,
+        hid_raw,
         vg,
         vp,
         lat_part,
@@ -143,9 +146,7 @@
     own_tok = [
         local(og.at[:, pl.ds(CHUNKS[k][0], CHUNKS[k][1])], tok[k].at[z], k) for k in range(N)
     ]
-    load_hid = [
-        local(hid.at[plane(d)], rows_out[1].at[:, :, i], N + 6) for i, d in enumerate(ORDER)
-    ]
+    load_hid = [local(hid, hid_raw, N + 6)]
     load_latent = [local(vgrad, vg, N), local(vproj, vp, N + 7)]
     load_meta = [local(routes, metas.at[z], N + 1), local(gates, gate_rows.at[z], N + 8)]
 
@@ -163,8 +164,7 @@
     for copy in load_hid + load_meta + own_tok[:1]:
         copy.start()
 
-    with jax.named_scope("barrier"):
-        pl.semaphore_wait(barrier, 17)
+    pl.semaphore_wait(barrier, 17)
 
     def meta_copies(i):
         return [
@@ -217,6 +217,10 @@
 
     def transpose_half(w):
         def piece(q, carry):
+            empty = jnp.zeros((POS - CAP, FPART), BF16)
+            for i, d in enumerate(ORDER):
+                rows_out[1][q, w, i, 0:CAP] = hid_raw[plane(d) * PEERS + q, :, w, :]
+                rows_out[1][q, w, i, CAP:POS] = empty
             hid_t[w, y, q] = rows_out[1][q, w].reshape(PLANES * POS, FPART).T
             return carry
 
@@ -229,7 +233,14 @@
         view = hid_t.at[w, y_part(part)]
         return remote(view, view, sem_hid.at[6], sem_hid.at[index], dev_y(d))
 
-    hid_copies = ((0, 0, 0, 1), (1, 1, 0, -1), (2, 1, 0, 1), (3, 0, 0, -1), (4, 0, -1, 1), (5, 1, 1, -1))
+    hid_copies = (
+        (0, 0, 0, 1),
+        (1, 1, 0, -1),
+        (2, 1, 0, 1),
+        (3, 0, 0, -1),
+        (4, 0, -1, 1),
+        (5, 1, 1, -1),
+    )
 
     def hid_send(index):
         hid_copy(*hid_copies[index]).start()
@@ -342,9 +353,16 @@
         if k >= 2:
             part_sent(k - 2)
 
+        matmul(k, 0, 1, 2, 3)
+        part_own(k).start()
+        others(lambda i: part_copy(k, peer(i)).start())
+
+    def matmul(k, *offsets):
+        dc = CHUNKS[k][1]
+
         def block(i, carry):
             w = lax.rem(i, 2)
-            part = lax.rem(y + i // 2, 4)
+            part = y_part(offsets[0] + i // 2)
             total = jnp.zeros((FPART, dc), F32)
             for q in range(PEERS):
                 total += jnp.dot(
@@ -358,9 +376,34 @@
                     part_out[k % 2, q, w, 2 * part + h, :, 0:dc] = rounded[h, q]
             return carry
 
-        lax.fori_loop(0, 8, block, 0)
-        part_own(k).start()
-        others(lambda i: part_copy(k, peer(i)).start())
+        lax.fori_loop(0, 2 * len(offsets), block, 0)
+
+    def piece_sends(d):
+        planes = pl.ds(2 * y_part(d), 2)
+
+        def send(i):
+            to = peer(i)
+            remote(
+                part_out.at[0, to, :, planes, :, pl.ds(0, CHUNKS[0][1])],
+                relay_x[0].at[:, p, planes],
+                sem_px.at[0, 0],
+                sem_px.at[1, 0],
+                dev_p(to),
+            ).start()
+
+        others(send)
+
+    def matmul_near():
+        rows_own(0).wait()
+        all_arrived(rows_in[0].at[:, 0:7], sem_rows.at[1, 0])
+        for d in (0, 1, -1):
+            matmul(0, d)
+            piece_sends(d)
+
+    def matmul_far():
+        matmul(0, 2)
+        piece_sends(2)
+        part_own(0).start()
 
     def grad_copy(k, to):
         return remote(
@@ -462,6 +505,9 @@
             dev_p(to),
         )
 
+    def plane_own(k, source):
+        return own(relay_s[k].at[:, source, p], out.at[:, source, p, :, columns(k)], 4, k)
+
     def stage_return(k):
         step_own(k).wait()
         if k < N - 2:
@@ -469,6 +515,7 @@
             out_own(k).start()
             others(lambda i: out_copy(k, peer(i)).start())
             return
+        plane_own(k, z).start()
         others(lambda i: plane_copy(k, z, peer(i)).start())
         for index in TURNS:
             source = plane(-index)
@@ -476,8 +523,8 @@
             remote(
                 view, view, sem_sz.at[0, k], sem_last.at[k - (N - 2), index], dev_z(source)
             ).wait_recv()
+            plane_own(k, source).start()
             others(lambda i: plane_copy(k, source, peer(i)).start())
-        out_own(k).start()
 
     def drain_start():
         all_sent(metas.at[0:7], sem_meta.at[0, 0])
@@ -540,209 +587,118 @@
     def hid_pass():
         hid_wait(0)
         hid_send(4)
-        hid_send(2)
         hid_wait(1)
         hid_send(5)
-        hid_send(3)
-
-    def hid_finish():
-        for index in (2, 3, 4, 5):
-            hid_wait(index)
-
-    with jax.named_scope("others"):
-        others(send_meta)
-    with jax.named_scope("ring_begin0"):
-        ring_begin(0)
-    with jax.named_scope("ring_begin1"):
-        ring_begin(1)
-    with jax.named_scope("wait_hid"):
-        wait_hid()
-    with jax.named_scope("transpose_half0"):
-        transpose_half(0)
-    with jax.named_scope("hid_send0"):
-        hid_send(0)
-    with jax.named_scope("transpose_half1"):
-        transpose_half(1)
-    with jax.named_scope("hid_send1"):
-        hid_send(1)
-    with jax.named_scope("late_loads"):
-        late_loads()
-    with jax.named_scope("prepare"):
-        prepare()
-    with jax.named_scope("meta_arrivals"):
-        meta_arrivals()
-    with jax.named_scope("build0"):
-        build(0)
-    with jax.named_scope("own_wait0"):
-        own_wait(0)
-    with jax.named_scope("pick00"):
-        pick(0, 0)
-    with jax.named_scope("build11"):
-        build(1, -1)
-    with jax.named_scope("ring_forward01"):
-        ring_forward(0, 1)
-    with jax.named_scope("pick011"):
-        pick(0, 1, -1)
-    with jax.named_scope("send_rows00"):
-        send_rows(0, 0)
-    with jax.named_scope("build22"):
-        build(2, -2)
-    with jax.named_scope("own_wait1"):
-        own_wait(1)
-    with jax.named_scope("pick10"):
-        pick(1, 0)
-    with jax.named_scope("ring_forward11"):
-        ring_forward(1, 1)
-    with jax.named_scope("pick111"):
-        pick(1, 1, -1)
-    with jax.named_scope("send_rows10"):
-        send_rows(1, 0)
-    with jax.named_scope("ring_forward02"):
-        ring_forward(0, 2)
-    with jax.named_scope("pick022"):
-        pick(0, 2, -2)
-    with jax.named_scope("send_rows01"):
-        send_rows(0, 1)
-    with jax.named_scope("build33"):
-        build(3, -3)
-    with jax.named_scope("hid_pass"):
-        hid_pass()
-    with jax.named_scope("ring_forward12"):
-        ring_forward(1, 2)
-    with jax.named_scope("pick122"):
-        pick(1, 2, -2)
-    with jax.named_scope("send_rows11"):
-        send_rows(1, 1)
-    with jax.named_scope("build4"):
-        build(4)
-    with jax.named_scope("build_kron"):
-        build_kron()
-    with jax.named_scope("ring_forward03"):
-        ring_forward(0, 3)
-    with jax.named_scope("ring_begin2"):
-        ring_begin(2)
-    with jax.named_scope("pick033"):
-        pick(0, 3, -3)
-    with jax.named_scope("ring_forward13"):
-        ring_forward(1, 3)
-    with jax.named_scope("ring_begin3"):
-        ring_begin(3)
-    with jax.named_scope("pick133"):
-        pick(1, 3, -3)
-    with jax.named_scope("ring_forward04"):
-        ring_forward(0, 4)
-    with jax.named_scope("pick04"):
-        pick(0, 4)
-    with jax.named_scope("send_rows02"):
-        send_rows(0, 2)
-    with jax.named_scope("ring_forward21"):
-        ring_forward(2, 1)
-    with jax.named_scope("own_wait2"):
-        own_wait(2)
-    with jax.named_scope("pick2011"):
-        pick(2, 0, 1, -1)
-    with jax.named_scope("send_rows20"):
-        send_rows(2, 0)
-    with jax.named_scope("ring_forward14"):
-        ring_forward(1, 4)
-    with jax.named_scope("pick14"):
-        pick(1, 4)
-    with jax.named_scope("send_rows12"):
-        send_rows(1, 2)
-    with jax.named_scope("ring_forward31"):
-        ring_forward(3, 1)
-    with jax.named_scope("own_wait3"):
-        own_wait(3)
-    with jax.named_scope("pick3011"):
-        pick(3, 0, 1, -1)
-    with jax.named_scope("ring_forward22"):
-        ring_forward(2, 2)
-    with jax.named_scope("pick222"):
-        pick(2, 2, -2)
-    with jax.named_scope("hid_finish"):
-        hid_finish()
-    with jax.named_scope("matmul0"):
-        stage_matmul(0)
-    with jax.named_scope("ring_forward32"):
-        ring_forward(3, 2)
-    with jax.named_scope("pick322"):
-        pick(3, 2, -2)
-    with jax.named_scope("matmul1"):
-        stage_matmul(1)
-    with jax.named_scope("ring_forward23"):
-        ring_forward(2, 3)
-    with jax.named_scope("pick233"):
-        pick(2, 3, -3)
-    with jax.named_scope("send_rows21"):
-        send_rows(2, 1)
-    with jax.named_scope("send_rows30"):
-        send_rows(3, 0)
-    with jax.named_scope("ring_forward33"):
-        ring_forward(3, 3)
-    with jax.named_scope("pick333"):
-        pick(3, 3, -3)
-    with jax.named_scope("forward0"):
-        stage_forward(0)
-    with jax.named_scope("ring_forward24"):
-        ring_forward(2, 4)
-    with jax.named_scope("pick24"):
-        pick(2, 4)
-    with jax.named_scope("send_rows22"):
-        send_rows(2, 2)
-    with jax.named_scope("send_rows31"):
-        send_rows(3, 1)
-    with jax.named_scope("ring_forward34"):
-        ring_forward(3, 4)
-    with jax.named_scope("pick34"):
-        pick(3, 4)
-    with jax.named_scope("send_rows32"):
-        send_rows(3, 2)
-    with jax.named_scope("forward1"):
-        stage_forward(1)
-    with jax.named_scope("latent_begin"):
-        latent_begin()
-    with jax.named_scope("matmul2"):
-        stage_matmul(2)
-    with jax.named_scope("matmul3"):
-        stage_matmul(3)
-    with jax.named_scope("adam0"):
-        stage_adam(0)
-    with jax.named_scope("forward2"):
-        stage_forward(2)
-    with jax.named_scope("forward3"):
-        stage_forward(3)
-    with jax.named_scope("adam1"):
-        stage_adam(1)
-    with jax.named_scope("return0"):
-        stage_return(0)
-    with jax.named_scope("latent_end"):
-        latent_end()
-    with jax.named_scope("adam2"):
-        stage_adam(2)
-    with jax.named_scope("drain_start"):
-        drain_start()
-    with jax.named_scope("return1"):
-        stage_return(1)
-    with jax.named_scope("adam3"):
-        stage_adam(3)
-    with jax.named_scope("drain_parts"):
-        drain_parts()
-    with jax.named_scope("return2"):
-        stage_return(2)
-    with jax.named_scope("drain_out0"):
-        drain_out(0)
-    with jax.named_scope("drain_out1"):
-        drain_out(1)
-    with jax.named_scope("step_sent2"):
-        step_sent(2)
-    with jax.named_scope("return3"):
-        stage_return(3)
-    with jax.named_scope("step_sent3"):
-        step_sent(3)
-    with jax.named_scope("drain_out2"):
-        drain_out(2)
-    with jax.named_scope("drain_out3"):
-        drain_out(3)
+
+    def hid_near():
+        hid_wait(2)
+        hid_wait(3)
+
+    def hid_far():
+        hid_wait(4)
+        hid_wait(5)
+
+    others(send_meta)
+    ring_begin(0)
+    ring_begin(1)
+    wait_hid()
+    transpose_half(0)
+    hid_send(0)
+    hid_send(3)
+    transpose_half(1)
+    hid_send(1)
+    hid_send(2)
+    late_loads()
+    prepare()
+    meta_arrivals()
+    build(0)
+    own_wait(0)
+    pick(0, 0)
+    build(1, -1)
+    ring_forward(0, 1)
+    pick(0, 1, -1)
+    send_rows(0, 0)
+    build(2, -2)
+    own_wait(1)
+    pick(1, 0)
+    ring_forward(1, 1)
+    pick(1, 1, -1)
+    send_rows(1, 0)
+    ring_forward(0, 2)
+    pick(0, 2, -2)
+    send_rows(0, 1)
+    build(3, -3)
+    ring_forward(1, 2)
+    pick(1, 2, -2)
+    send_rows(1, 1)
+    build(4)
+    build_kron()
+    ring_forward(0, 3)
+    ring_begin(2)
+    pick(0, 3, -3)
+    ring_forward(1, 3)
+    ring_begin(3)
+    pick(1, 3, -3)
+    hid_pass()
+    ring_forward(0, 4)
+    pick(0, 4)
+    send_rows(0, 2)
+    ring_forward(2, 1)
+    own_wait(2)
+    pick(2, 0, 1, -1)
+    ring_forward(1, 4)
+    pick(1, 4)
+    ring_forward(3, 1)
+    hid_near()
+    matmul_near()
+    send_rows(1, 2)
+    ring_forward(2, 2)
+    pick(2, 2, -2)
+    ring_forward(3, 2)
+    hid_far()
+    matmul_far()
+    own_wait(3)
+    pick(3, 0, 1, -1)
+    ring_forward(2, 3)
+    stage_matmul(1)
+    send_rows(2, 0)
+    ring_forward(3, 3)
+    stage_forward(0)
+    pick(3, 2, -2)
+    pick(2, 3, -3)
+    send_rows(2, 1)
+    send_rows(3, 0)
+    pick(3, 3, -3)
+    send_rows(3, 1)
+    ring_forward(2, 4)
+    pick(2, 4)
+    send_rows(2, 2)
+    ring_forward(3, 4)
+    pick(3, 4)
+    send_rows(3, 2)
+    stage_forward(1)
+    latent_begin()
+    stage_adam(0)
+    stage_matmul(2)
+    stage_matmul(3)
+    stage_forward(2)
+    stage_forward(3)
+    stage_adam(1)
+    stage_return(0)
+    latent_end()
+    stage_adam(2)
+    drain_start()
+    stage_return(1)
+    stage_adam(3)
+    drain_parts()
+    stage_return(2)
+    drain_out(0)
+    drain_out(1)
+    step_sent(2)
+    stage_return(3)
+    step_sent(3)
+    drain_out(2)
+    drain_out(3)
 
 
 def expert_steps(*operands):
@@ -751,7 +707,7 @@
         jax.ShapeDtypeStruct((2, PEERS, PLANES, ROWS, dc), BF16) for _, dc in CHUNKS
     ]
     returns = [
-        jax.ShapeDtypeStruct((2, PLANES, PEERS, ROWS, dc), BF16) for _, dc in CHUNKS
+        jax.ShapeDtypeStruct((2, PLANES, PEERS, ROWS, dc), BF16) for _, dc in CHUNKS[: N - 2]
     ]
     shape = jax.ShapeDtypeStruct((2, PLANES, PEERS, ROWS, WIDTH), BF16)
     widest = max(dc for _, dc in CHUNKS)
@@ -760,6 +716,7 @@
     scratch += [pltpu.VMEM((2, PEERS, PLANES, POS, dc), BF16) for _, dc in CHUNKS]
     scratch += [pltpu.VMEM((2, PLANES, PEERS, ROWS, dc), BF16) for _, dc in CHUNKS]
     scratch += [pltpu.VMEM((PEERS, 2, PLANES, POS, dc), BF16) for _, dc in CHUNKS]
+    scratch += [pltpu.VMEM((2, PLANES, PEERS, ROWS, dc), BF16) for _, dc in CHUNKS[N - 2 :]]
     scratch += [
         pltpu.VMEM((PLANES, 4, TOKENS), jnp.int32),
         pltpu.VMEM((PLANES, 4, TOKENS), F32),
@@ -772,6 +729,7 @@
         pltpu.VMEM((1024, 1024), BF16),
         pltpu.VMEM((1024, 1024), BF16),
         pltpu.VMEM((TOKENS, TOKENS), BF16),
+        pltpu.VMEM((PLANES * PEERS, CAP, 2, FPART), BF16),
         pltpu.VMEM((TOKENS, 1024), BF16),
         pltpu.VMEM((512, 1024), BF16),
         pltpu.VMEM((4, 128, TOKENS), F32),
@@ -794,7 +752,7 @@
         kernel,
         out_shape=[shape, jax.ShapeDtypeStruct((128, TOKENS), BF16)] + relays + returns,
         in_specs=[anywhere] * 4 + [pl.BlockSpec(memory_space=pltpu.VMEM)] + [anywhere] * 4,
-        out_specs=[anywhere] * (2 + 2 * N),
+        out_specs=[anywhere] * (2 * N),
         scratch_shapes=scratch,
         compiler_params=pltpu.CompilerParams(
             collective_id=0, has_side_effects=True, vmem_limit_bytes=62 * 1024 * 1024
@@ -806,10 +764,43 @@
     return results[0], results[1]
 
 
+def hand_over_kernel(steps, latent, steps_out, latent_out, steps_held, latent_held, sem):
+    pieces = [
+        (steps.at[w, i], steps_held.at[w, i], steps_out.at[w, i])
+        for w in range(2)
+        for i in range(PLANES)
+    ]
+    pieces.append((latent, latent_held, latent_out))
+    into = [
+        pltpu.make_async_copy(a, b, sem.at[0, n]) for n, (a, b, _) in enumerate(pieces)
+    ]
+    back = [
+        pltpu.make_async_copy(b, c, sem.at[1, n]) for n, (_, b, c) in enumerate(pieces)
+    ]
+    for copy in into:
+        copy.start()
+    for first, second in zip(into, back):
+        first.wait()
+        second.start()
+    for copy in back:
+        copy.wait()
+
+
+def hand_over(*results):
+    anywhere = pl.BlockSpec(memory_space=pl.ANY)
+    return pl.pallas_call(
+        hand_over_kernel,
+        out_shape=[jax.ShapeDtypeStruct(r.shape, r.dtype) for r in results],
+        in_specs=[anywhere] * 2,
+        out_specs=[anywhere] * 2,
+        scratch_shapes=[pltpu.VMEM(r.shape, r.dtype) for r in results]
+        + [pltpu.SemaphoreType.DMA((2, 2 * PLANES + 1))],
+    )(*results)
+
+
 def shards(out_grad, routes, gates, dup_owner, hidden, moment1, moment2, value_grad, value_proj):
     experts = PLANES * PEERS
-    hid = jnp.pad(hidden[0], ((0, 0), (0, 0), (0, POS - hidden.shape[3]), (0, 0)))
-    hid = hid.reshape(PLANES, PEERS, 2, POS, FPART)
+    hid = hidden[0].transpose(0, 2, 1, 3)
     steps, latent_grad = expert_steps(
         out_grad,
         routes.T,
@@ -821,6 +812,7 @@
         value_grad,
         value_proj,
     )
+    steps, latent_grad = hand_over(steps, latent_grad)
     return (steps.reshape(1, 2, PLANES * PEERS * ROWS, WIDTH), latent_grad)
 
 

time: 278 us -> 271 us (0.975)
  local copies, waits for them, and re-layouts: 8.45 us -> 0 us
    unnamed x5 -> x0, local copies, waits for them, and re-layouts: 6.86 us -> none
    pallas_call x0 -> x1, Pallas kernels: none -> 3.93 us  [hand_over(): pl.pallas_call(hand_over_kernel, out_shape=[jax.ShapeDtypeStruct(r.shape,...]
    pallas_call x1, Pallas kernels: 269 us -> 266 us  [expert_steps(): pl.pallas_call(kernel, out_shape=[shape, jax.ShapeDtypeStruct((128, TOKEN...]
where the time goes in v3:
time: 271 us
  Pallas kernels  270 us (100%)
    pallas_call x1, Pallas kernels, expert_steps(): pl.pallas_call(kernel, out_shape=[shape, jax.ShapeDtypeStruct((128, TOKEN...  266 us

profile of v3, /device:TPU:1, one launch (start us, length us, event | category | flops | bytes accessed | tf_op | source)
XLA Modules:
  0.0 270.7 jit_solution(5323540287697420908)
XLA Ops:
  0.6 266.0 %shard_map.104 = (bf16[2,8,8,16,896]{4,3,2,1,0:T(8,128)(2,1)}, bf16[128,640]{1,0:T(8,128)(2,1)}, bf16[2,8,8,16,256]{4,3,2,1,0:T(8,128)(2,1)}, bf16[2,8,8,16,256]...) custom-call(bf16[640,896]{1,0:T(8,128)(2,1)} %og.1, ...), custom_call_target="tpu_custom_call" | custom-call | flops 49999998976 | bytes 60000000 | tf_op jit(solution)/shard_map/pallas_call | solution.py:751
  266.6 3.9 %shard_map.105 = (bf16[2,8,8,16,896]{4,3,2,1,0:T(8,128)(2,1)}, bf16[128,640]{1,0:T(8,128)(2,1)}) custom-call(bf16[2,8,8,16,896]{4,3,2,1,0:T(8,128)(2,1)} %get-tuple-element.6.steps, bf16[128,640]{1,0:T(8,128)(2,1)} %get-tuple-element.7.latent), custom_call_target="tpu_custom_call" | custom-call | tf_op jit(solution)/shard_map/pallas_call | solution.py:791

commit v4 on v3

--- a/solution.py
+++ b/solution.py
@@ -26,6 +26,7 @@
 ORDER = (0, 1, -1, 2, -2, 3, -3, 4)
 GROUPS = ((0, 3), (3, 5), (5, 8))
 HALF = TOKENS // 2
+NEED = 16 * CAP
 TURNS = (1, 7, 2, 6, 3, 5, 4)
 MESH = pl.DeviceIdType.MESH
 F32 = jnp.float32
@@ -46,16 +47,17 @@
     latent,
     *refs,
 ):
-    relay_x, relay_s, refs = refs[:N], list(refs[N : 2 * N - 2]), refs[2 * N - 2 :]
+    relay_x, relay_s, refs = refs[:N], list(refs[N : 2 * N - 1]), refs[2 * N - 1 :]
     tok, refs = refs[:N], refs[N:]
     rows_in, refs = refs[:N], refs[N:]
     grad_in, refs = refs[:N], refs[N:]
     rows_out, refs = refs[:N], refs[N:]
-    relay_s, refs = relay_s + list(refs[:2]), refs[2:]
+    relay_s, refs = relay_s + list(refs[:1]), refs[1:]
     (
         metas,
         gate_rows,
         onehot,
+        onehot_kept,
         gate_col,
         hid_t,
         part_out,
@@ -183,37 +185,69 @@
             for copy in load_moments(k):
                 copy.start()
 
+    def last_step(k, way):
+        return 4 if way == k % 2 else 3
+
+    def ring_rows(k, way, step, half):
+        size = HALF if step < last_step(k, way) else NEED // 2
+        return pl.ds(half * size, size)
+
+    def ring_sent(k, way, step):
+        return sem_ring_sent.at[0 if step < last_step(k, way) else 1, k]
+
     def ring_send(k, way, step, half):
         c0, dc = CHUNKS[k]
         sign = 1 - 2 * way
         block = plane(-sign * (step - 1))
-        rows = pl.ds(half * HALF, HALF)
+        rows = ring_rows(k, way, step, half)
         source = og.at[rows, pl.ds(c0, dc)] if step == 1 else tok[k].at[block, rows]
         arrived = sem_ring.at[k, way, step - 1, half]
         return remote(
-            source, tok[k].at[block, rows], sem_ring_sent.at[k], arrived, dev_z(plane(sign))
+            source, tok[k].at[block, rows], ring_sent(k, way, step), arrived, dev_z(plane(sign))
         )
 
     def ring_arrival(k, way, step, half):
         sign = 1 - 2 * way
-        block = plane(-sign * step)
-        rows = pl.ds(half * HALF, HALF)
+        view = tok[k].at[plane(-sign * step), ring_rows(k, way, step, half)]
         arrived = sem_ring.at[k, way, step - 1, half]
-        view = tok[k].at[block, rows]
-        return remote(view, view, sem_ring_sent.at[k], arrived, dev_z(plane(sign)))
-
-    def ring_parts(step):
-        return [(way, half) for half in (0, 1) for way in (0, 1) if step < 4 or half == way]
+        return remote(view, view, ring_sent(k, way, step), arrived, dev_z(plane(sign)))
 
     def ring_begin(k):
-        for way, half in ring_parts(1):
-            ring_send(k, way, 1, half).start()
+        for half in (0, 1):
+            for way in (0, 1):
+                ring_send(k, way, 1, half).start()
 
     def ring_forward(k, step):
-        for way, half in ring_parts(step):
-            ring_arrival(k, way, step, half).wait_recv()
-            if step < 3 or (step == 3 and half == way):
-                ring_send(k, way, step + 1, half).start()
+        ways = [way for way in (0, 1) if step <= last_step(k, way)]
+        for half in (0, 1):
+            for way in ways:
+                ring_arrival(k, way, step, half).wait_recv()
+                if step + 1 < last_step(k, way):
+                    ring_send(k, way, step + 1, half).start()
+        for way in ways:
+            if step + 1 == last_step(k, way):
+                sign = 1 - 2 * way
+                gather(k, -sign * step)
+                block = plane(-sign * step)
+                chosen = selection(needed(block, plane(sign)))
+                kept = jnp.dot(chosen, tok[k][block], preferred_element_type=F32)
+                tok[k][block, 0:NEED] = kept.astype(BF16)
+                for half in (0, 1):
+                    ring_send(k, way, step + 1, half).start()
+
+    def needed(group, of_plane):
+        match = jnp.where(lax.shift_right_logical(metas[group], 4) == of_plane, 1.0, 0.0)
+        return jnp.max(match, axis=0, keepdims=True)
+
+    def selection(need):
+        before = jnp.dot(
+            jnp.broadcast_to(need, (16, TOKENS)).astype(BF16),
+            earlier[...],
+            preferred_element_type=F32,
+        )
+        place = jnp.where(need > 0.5, before[0:1, :], -1.0)
+        position = lax.broadcasted_iota(jnp.int32, (NEED, TOKENS), 0).astype(F32)
+        return jnp.where(position == place, 1.0, 0.0).astype(BF16)
 
     def transpose_half(w):
         def piece(q, carry):
@@ -249,7 +283,8 @@
         number, w, part, d = hid_copies[index]
         hid_copy(number, w, part - d, d).wait_recv()
 
-    def build_plane(i):
+    def build_plane(d):
+        i = plane(d)
         slot_of = lax.broadcasted_iota(jnp.int32, (16, TOKENS), 0) + z * 16
         named = jnp.zeros((16, TOKENS), F32)
         gate = jnp.zeros((16, TOKENS), F32)
@@ -267,15 +302,36 @@
                 jnp.where(chosen, gate[s : s + 1, :], 0.0), axis=1, keepdims=True
             )
             gate_col[i, s * POS : (s + 1) * POS, :] = jnp.broadcast_to(weight, (POS, 128))
+        if abs(d) >= 3:
+            kept = lax.dot_general(
+                (rank + 1.0).astype(BF16),
+                selection(needed(i, z)),
+                (((1,), (1,)), ((), ())),
+                preferred_element_type=F32,
+            )
+            kept = kept - 1.0
+            position = lax.broadcasted_iota(jnp.int32, (POS, NEED), 0).astype(F32)
+            for s in range(16):
+                chosen = jnp.where(position == kept[s : s + 1, :], 1.0, 0.0).astype(BF16)
+                if d == 4:
+                    onehot[i, s * POS : (s + 1) * POS, 0:NEED] = chosen
+                else:
+                    onehot_kept[(d + 3) // 6, s * POS : (s + 1) * POS, :] = chosen
 
     def build(*distances):
         for d in distances:
-            build_plane(plane(d))
+            build_plane(d)
 
     def gather(k, d):
         dc = CHUNKS[k][1]
         source, place = plane(d), ORDER.index(d)
-        picked = jnp.dot(onehot[source], tok[k][source], preferred_element_type=F32)
+        if d == 4:
+            picks, rows = onehot[source, :, 0:NEED], tok[k][source, 0:NEED]
+        elif d == (3 if k % 2 == 0 else -3):
+            picks, rows = onehot_kept[(d + 3) // 6], tok[k][source, 0:NEED]
+        else:
+            picks, rows = onehot[source], tok[k][source]
+        picked = jnp.dot(picks, rows, preferred_element_type=F32)
         for part in range(dc // 128):
             lanes = slice(part * 128, (part + 1) * 128)
             scaled = (picked[:, lanes] * gate_col[source]).astype(BF16)
@@ -298,8 +354,10 @@
         return own(rows_out[k].at[p], rows_in[k].at[:, p], 0, k)
 
     def pick(k, *distances):
+        ahead = (-3, 2) if k % 2 == 0 else (3, -2)
         for d in distances:
-            gather(k, d)
+            if d not in ahead:
+                gather(k, d)
 
     def send_rows(k, group):
         others(lambda i: rows_copy(k, group, peer(i)).start())
@@ -532,7 +590,8 @@
         all_sent(hid_t.at[:, 0:3], sem_hid.at[6])
         all_sent(lat_in, sem_lat.at[0])
         for k in range(N):
-            all_sent(tok[k].at[0:7], sem_ring_sent.at[k])
+            all_sent(tok[k].at[0:5], sem_ring_sent.at[0, k])
+            all_sent(tok[k].at[0:2, 0:NEED], sem_ring_sent.at[1, k])
             all_sent(rows_out[k].at[0:7], sem_rows.at[0, k])
 
     def drain_parts():
@@ -707,7 +766,7 @@
         jax.ShapeDtypeStruct((2, PEERS, PLANES, ROWS, dc), BF16) for _, dc in CHUNKS
     ]
     returns = [
-        jax.ShapeDtypeStruct((2, PLANES, PEERS, ROWS, dc), BF16) for _, dc in CHUNKS[: N - 2]
+        jax.ShapeDtypeStruct((2, PLANES, PEERS, ROWS, dc), BF16) for _, dc in CHUNKS[: N - 1]
     ]
     shape = jax.ShapeDtypeStruct((2, PLANES, PEERS, ROWS, WIDTH), BF16)
     widest = max(dc for _, dc in CHUNKS)
@@ -716,11 +775,12 @@
     scratch += [pltpu.VMEM((2, PEERS, PLANES, POS, dc), BF16) for _, dc in CHUNKS]
     scratch += [pltpu.VMEM((2, PLANES, PEERS, ROWS, dc), BF16) for _, dc in CHUNKS]
     scratch += [pltpu.VMEM((PEERS, 2, PLANES, POS, dc), BF16) for _, dc in CHUNKS]
-    scratch += [pltpu.VMEM((2, PLANES, PEERS, ROWS, dc), BF16) for _, dc in CHUNKS[N - 2 :]]
+    scratch += [pltpu.VMEM((2, PLANES, PEERS, ROWS, dc), BF16) for _, dc in CHUNKS[N - 1 :]]
     scratch += [
         pltpu.VMEM((PLANES, 4, TOKENS), jnp.int32),
         pltpu.VMEM((PLANES, 4, TOKENS), F32),
         pltpu.VMEM((PLANES, 16 * POS, TOKENS), BF16),
+        pltpu.VMEM((2, 16 * POS, NEED), BF16),
         pltpu.VMEM((PLANES, 16 * POS, 128), F32),
         pltpu.VMEM((2, 4, PEERS, FPART, PLANES * POS), BF16),
         pltpu.VMEM((2, PEERS, 2, PLANES, ROWS, widest), BF16),
@@ -736,7 +796,7 @@
         pltpu.VMEM((3, 128, TOKENS), F32),
         dma((2, 2)),
         dma((N, 2, 4, 2)),
-        dma((N,)),
+        dma((2, N)),
         dma((7,)),
         dma((2, N)),
         dma((2, N)),
@@ -752,7 +812,7 @@
         kernel,
         out_shape=[shape, jax.ShapeDtypeStruct((128, TOKENS), BF16)] + relays + returns,
         in_specs=[anywhere] * 4 + [pl.BlockSpec(memory_space=pltpu.VMEM)] + [anywhere] * 4,
-        out_specs=[anywhere] * (2 * N),
+        out_specs=[anywhere] * (2 * N + 1),
         scratch_shapes=scratch,
         compiler_params=pltpu.CompilerParams(
             collective_id=0, has_side_effects=True, vmem_limit_bytes=62 * 1024 * 1024

time: 271 us -> 268 us (0.989)
  Pallas kernels: 270 us -> 266 us
    pallas_call x1, Pallas kernels: 266 us -> 262 us  [expert_steps(): pl.pallas_call(kernel, out_shape=[shape, jax.ShapeDtypeStruct((128, TOKEN...]
where the time goes in v4:
time: 268 us; the launch traced here: 267 us
  Pallas kernels  266 us (99%)
    pallas_call x1, Pallas kernels, expert_steps(): pl.pallas_call(kernel, out_shape=[shape, jax.ShapeDtypeStruct((128, TOKEN...  262 us

profile of v4, /device:TPU:1, one launch (start us, length us, event | category | flops | bytes accessed | tf_op | source)
XLA Modules:
  0.0 266.7 jit_solution(2480705622464796340)
XLA Ops:
  0.6 262.0 %shard_map.104 = (bf16[2,8,8,16,896]{4,3,2,1,0:T(8,128)(2,1)}, bf16[128,640]{1,0:T(8,128)(2,1)}, bf16[2,8,8,16,256]{4,3,2,1,0:T(8,128)(2,1)}, bf16[2,8,8,16,256]...) custom-call(bf16[640,896]{1,0:T(8,128)(2,1)} %og.1, ...), custom_call_target="tpu_custom_call" | custom-call | flops 49999998976 | bytes 60000000 | tf_op jit(solution)/shard_map/pallas_call | solution.py:811
  262.6 3.9 %shard_map.105 = (bf16[2,8,8,16,896]{4,3,2,1,0:T(8,128)(2,1)}, bf16[128,640]{1,0:T(8,128)(2,1)}) custom-call(bf16[2,8,8,16,896]{4,3,2,1,0:T(8,128)(2,1)} %get-tuple-element.6.steps, bf16[128,640]{1,0:T(8,128)(2,1)} %get-tuple-element.7.latent), custom_call_target="tpu_custom_call" | custom-call | tf_op jit(solution)/shard_map/pallas_call | solution.py:851

commit v5 on v4

--- a/solution.py
+++ b/solution.py
@@ -710,19 +710,19 @@
     ring_forward(3, 1)
     hid_near()
     matmul_near()
+    ring_forward(2, 2)
+    hid_far()
+    matmul_far()
     send_rows(1, 2)
-    ring_forward(2, 2)
     pick(2, 2, -2)
     ring_forward(3, 2)
-    hid_far()
-    matmul_far()
     own_wait(3)
     pick(3, 0, 1, -1)
     ring_forward(2, 3)
+    stage_forward(0)
+    ring_forward(3, 3)
     stage_matmul(1)
     send_rows(2, 0)
-    ring_forward(3, 3)
-    stage_forward(0)
     pick(3, 2, -2)
     pick(2, 3, -3)
     send_rows(2, 1)
@@ -732,10 +732,10 @@
     ring_forward(2, 4)
     pick(2, 4)
     send_rows(2, 2)
+    stage_forward(1)
     ring_forward(3, 4)
     pick(3, 4)
     send_rows(3, 2)
-    stage_forward(1)
     latent_begin()
     stage_adam(0)
     stage_matmul(2)

time: 268 us -> 267 us (level)
  no operation moved by 1% of the time
where the time goes in v5:
time: 267 us; the launch traced here: 266 us
  Pallas kernels  266 us (100%)
    pallas_call x1, Pallas kernels, expert_steps(): pl.pallas_call(kernel, out_shape=[shape, jax.ShapeDtypeStruct((128, TOKEN...  262 us

profile of v5, /device:TPU:1, one launch (start us, length us, event | category | flops | bytes accessed | tf_op | source)
XLA Modules:
  0.0 266.4 jit_solution(964535811434193109)
XLA Ops:
  0.6 261.7 %shard_map.104 = (bf16[2,8,8,16,896]{4,3,2,1,0:T(8,128)(2,1)}, bf16[128,640]{1,0:T(8,128)(2,1)}, bf16[2,8,8,16,256]{4,3,2,1,0:T(8,128)(2,1)}, bf16[2,8,8,16,256]...) custom-call(bf16[640,896]{1,0:T(8,128)(2,1)} %og.1, ...), custom_call_target="tpu_custom_call" | custom-call | flops 49999998976 | bytes 60000000 | tf_op jit(solution)/shard_map/pallas_call | solution.py:811
  262.3 3.9 %shard_map.105 = (bf16[2,8,8,16,896]{4,3,2,1,0:T(8,128)(2,1)}, bf16[128,640]{1,0:T(8,128)(2,1)}) custom-call(bf16[2,8,8,16,896]{4,3,2,1,0:T(8,128)(2,1)} %get-tuple-element.6.steps, bf16[128,640]{1,0:T(8,128)(2,1)} %get-tuple-element.7.latent), custom_call_target="tpu_custom_call" | custom-call | tf_op jit(solution)/shard_map/pallas_call | solution.py:851

commit v6 on v5

--- a/solution.py
+++ b/solution.py
@@ -740,9 +740,9 @@
     stage_adam(0)
     stage_matmul(2)
     stage_matmul(3)
+    stage_adam(1)
     stage_forward(2)
     stage_forward(3)
-    stage_adam(1)
     stage_return(0)
     latent_end()
     stage_adam(2)

time: 267 us -> 267 us (level)
  no operation moved by 1% of the time
where the time goes in v6:
time: 267 us
  Pallas kernels  266 us (100%)
    pallas_call x1, Pallas kernels, expert_steps(): pl.pallas_call(kernel, out_shape=[shape, jax.ShapeDtypeStruct((128, TOKEN...  262 us

profile of v6, /device:TPU:1, one launch (start us, length us, event | category | flops | bytes accessed | tf_op | source)
XLA Modules:
  0.0 266.5 jit_solution(4154248837891955735)
XLA Ops:
  0.6 261.8 %shard_map.104 = (bf16[2,8,8,16,896]{4,3,2,1,0:T(8,128)(2,1)}, bf16[128,640]{1,0:T(8,128)(2,1)}, bf16[2,8,8,16,256]{4,3,2,1,0:T(8,128)(2,1)}, bf16[2,8,8,16,256]...) custom-call(bf16[640,896]{1,0:T(8,128)(2,1)} %og.1, ...), custom_call_target="tpu_custom_call" | custom-call | flops 49999998976 | bytes 60000000 | tf_op jit(solution)/shard_map/pallas_call | solution.py:811
  262.4 3.9 %shard_map.105 = (bf16[2,8,8,16,896]{4,3,2,1,0:T(8,128)(2,1)}, bf16[128,640]{1,0:T(8,128)(2,1)}) custom-call(bf16[2,8,8,16,896]{4,3,2,1,0:T(8,128)(2,1)} %get-tuple-element.6.steps, bf16[128,640]{1,0:T(8,128)(2,1)} %get-tuple-element.7.latent), custom_call_target="tpu_custom_call" | custom-call | tf_op jit(solution)/shard_map/pallas_call | solution.py:851
